TPU v7x, 1024 devices: a whole 4x4x32 slice. The times are simulated.
1024 devices in a mesh: zone: 64 (over z, core), level: 16 (over x, y).
Axes of the slice: x: 4, y: 4, z: 32, core: 2. Of those that a mesh axis runs over, the one named last changes fastest.
Arguments:
- multipoles: bfloat16 [16384, 121], P(('zone', 'level')), may hold values from -6 to 6
- operators: bfloat16 [189, 121, 121], replicated, may hold values from -0.0390625 to 0.0390625
- parent_locals: float32 [2048, 121], P(('zone', 'level')), may hold values from -6 to 6
- shifts: float32 [8, 121, 121], replicated, may hold values from -0.5 to 0.5
- send_slots: int32 [1024, 64, 4], P(('zone', 'level')), may hold values from -1 to 15, as said below
- lists: int32 [16384, 189], P(('zone', 'level')), may hold values from -1 to 271, as said below
- positions: float32 [16384, 3, 256], P(('zone', 'level')), may hold values from 0 to 544, as said below
- charges: float32 [16384, 256], P(('zone', 'level')), may hold values from -0.09 to 0.09
- counts: int32 [16384], P(('zone', 'level')), may hold values from 64 to 256
- near_lists: int32 [16384, 27], P(('zone', 'level')), may hold values from -1 to 47, as said below
Outputs:
- local_coeffs: float32 [16384, 121], P(('zone', 'level'))
- potential: float32 [16384, 256], P(('zone', 'level'))
Inputs may be any that keep to these rules, and one draw needn't show every extreme that they name: `send_slots`: A tile's non-empty slots toward a reader zone come first; each tile fills all 4 slots toward some zones and 1 to 4 toward others. `lists`: an entry of 16 or more always names a non-empty slot. `near_lists`: the first entry of each box names the box itself; the others name, in an order drawn for each box, some of the boxes whose cubes touch its cube among the same zone's groups l - 1, l, l + 1 (which ones is drawn), and -1 elsewhere; box n is in the list of box b exactly when b is in the list of n. `positions`: each box's particles lie in its own cube of side 0.5; a group's boxes form one layer of cubes in Morton order, a zone's groups are stacked layers.
All inputs are finite; a program needn't handle non-finite values.
Results may differ from a plain program's by a relative error of at most 0.0003.
Values may be sent and summed in bfloat16 or wider, within the bound.
A program may use at most 32 MiB of HBM per device.

v0:
```python
import jax
import jax.numpy as jnp
from jax import lax
from jax.sharding import PartitionSpec as P

soften = 0.0025


def padded(cells, sides, width):
    for axis, dim in sides:
        count = lax.axis_size(axis)
        ends = count - 1
        head = lax.slice_in_dim(cells, 0, width, axis=dim)
        tail = lax.slice_in_dim(cells, cells.shape[dim] - width, cells.shape[dim], axis=dim)
        cells = jnp.concatenate(
            [
                lax.ppermute(tail, axis, [(i, (i + 1) % count) for i in range(ends)]),
                cells,
                lax.ppermute(head, axis, [((i + 1) % count, i) for i in range(ends)]),
            ],
            axis=dim,
        )
    return cells


def pair_kernel(targets, sources, self_pair):
    distance = soften
    for component in range(3):
        offset = targets[:, component, :, None] - sources[:, component, None, :]
        distance = distance + offset * offset
    kernel = lax.rsqrt(distance)
    return jnp.where(self_pair, 0.0, kernel)


def near_field(window, near_rows, occupied_rows, box_dev):
    slot_count = window.shape[2]
    targets = window[box_dev : 2 * box_dev]
    own_index = jnp.arange(box_dev, dtype=jnp.int32) + box_dev
    diagonal = jnp.arange(slot_count)[:, None] == jnp.arange(slot_count)[None, :]

    def one_member(column, running):
        list_entry = near_rows[:, column]
        present = list_entry >= 0
        sources = window[jnp.maximum(list_entry, 0)]
        self_pair = (list_entry == own_index)[:, None, None] & diagonal[None]
        kernel = pair_kernel(targets, sources, self_pair)
        partial_sum = jnp.sum(kernel * sources[:, 3, None, :], axis=2)
        return running + jnp.where(present[:, None], partial_sum, 0.0)

    running = lax.fori_loop(
        0, near_rows.shape[1], one_member, jnp.zeros((box_dev, slot_count), jnp.float32)
    )
    return jnp.where(occupied_rows, running, 0.0)


def per_device(
    multipoles,
    operators,
    parent_locals,
    shifts,
    send_slots,
    lists,
    positions,
    charges,
    counts,
    near_lists,
):
    box_dev = multipoles.shape[0]
    coefficients = multipoles.shape[1]
    capacity = send_slots.shape[2]
    slot_rows = jnp.arange(charges.shape[1], dtype=jnp.int32)
    occupied = slot_rows[None, :] < counts[:, None]
    charged = jnp.where(occupied, charges, 0.0)
    packed = jnp.concatenate([positions, charged[:, None, :]], axis=1)
    window = padded(packed, (("level", 0),), box_dev)
    potential = near_field(window, near_lists, occupied, box_dev)
    present = lists >= 0
    outgoing = send_slots[0]
    slot_boxes = lax.all_to_all(outgoing, "zone", split_axis=0, concat_axis=0, tiled=True)
    everything = lax.all_gather(multipoles, "zone", axis=0, tiled=True)
    my_zone = lax.axis_index("zone")
    remote = jnp.maximum(lists - box_dev, 0)
    peer_zone = remote // capacity
    slot_index = remote % capacity
    remote_box = slot_boxes[peer_zone, slot_index]
    row_index = jnp.where(
        lists < box_dev, my_zone * box_dev + lists, peer_zone * box_dev + remote_box
    )
    row_index = jnp.where(present, row_index, 0)
    gathered = everything[row_index]
    gathered = jnp.where(present[:, :, None], gathered, jnp.zeros((), gathered.dtype))
    far_field = jnp.dot(
        gathered.reshape(box_dev, -1),
        operators.reshape(-1, coefficients),
        preferred_element_type=jnp.float32,
    )
    downward = jnp.einsum(
        "gp,cpq->gcq", parent_locals, shifts, precision=lax.Precision.HIGHEST
    ).reshape(box_dev, coefficients)
    local_coeffs = far_field + downward
    return (local_coeffs, potential)


def solution(mesh):
    placed = (
        P(("zone", "level"), None),
        P(),
        P(("zone", "level"), None),
        P(),
        P(("zone", "level"), None, None),
        P(("zone", "level"), None),
        P(("zone", "level"), None, None),
        P(("zone", "level"), None),
        P(("zone", "level")),
        P(("zone", "level"), None),
    )
    return jax.shard_map(
        per_device,
        mesh=mesh,
        in_specs=placed,
        out_specs=(P(("zone", "level"), None), P(("zone", "level"), None)),
        check_vma=False,
    )
```

profile of v0, /device:TPU:1, one launch (start us, length us, event | category | flops | bytes accessed | tf_op | source)
XLA Modules:
  0.0 259.7 jit_solution(4004702047931805924)
XLA Ops:
  3.7 4.7 %collective-permute-start = (f32[16,4,256]{2,1,0:T(4,128)S(1)}, f32[16,4,256]{2,1,0:T(4,128)S(1)}, u32[]{:S(2)}, u32[]{:S(2)}) collective-permute-start(f32[16,4,256]{2,1,0:T(4,128)S(1)} %pad_maximum_fusion.1), channel_id=1, source_target_pairs={{0,1},{1,2},{2,3},{3,4},{4,5},{5,6},{6,7},{7,8},{8,9},{9,10},{10,1... | collective-permute-start | bytes 196616 | tf_op jit(solution)/shard_map/ppermute | solution.py:17
  9.8 30.3 %all-to-all-start = ((s32[64,1,4]{2,1,0:T(1,128)}), s32[64,1,4]{2,1,0:T(1,128)S(1)}, u32[]{:S(2)}, u32[]{:S(2)}) async-start(s32[64,1,4]{2,1,0:T(1,128)} %bitcast), calls=%async_computation | async-start | bytes 65536 | tf_op jit(solution)/shard_map/all_to_all | solution.py:79
  42.6 57.9 %all_gather.3 = bf16[1024,121]{1,0:T(8,128)(2,1)S(1)} all-gather(bf16[16,121]{1,0:T(8,128)(2,1)} %param.12), channel_id=1, replica_groups=mesh['zone'=64,'level'=16] {'zone'}, dimensions={0}, use_global_device_ids=true | all-gather | bytes 251680 | tf_op jit(solution)/shard_map/all_gather | solution.py:80
  101.5 37.5 %gather_fusion.1 = s32[3024]{0:T(1024)S(1)} fusion(s32[64,4]{0,1:T(4,128)S(1)} %bitcast.47, s32[3024]{0:T(1024)S(1)} %reshape.38), kind=kCustom, calls=%fused_computation.1 | custom fusion | bytes 48384 | tf_op jit(solution)/shard_map/gather | solution.py:85
  139.3 9.3 %gather_fusion.2 = bf16[3024,121]{1,0:T(8,128)(2,1)S(1)} fusion(bf16[1024,121]{1,0:T(8,128)(2,1)S(1)} %all_gather.3, s32[3072]{0:T(1024)S(1)} %pad_clamp_fusion.1), kind=kCustom, calls=%fused_computation.2 | custom fusion | bytes 1475712 | tf_op jit(solution)/shard_map/gather | solution.py:90
  150.3 4.3 %fusion.4 = f32[16,121]{1,0:T(8,128)} fusion(bf16[16,189,121]{1,0,2:T(8,128)(2,1)S(1)} %copy.37, bf16[189,121,121]{2,0,1:T(8,128)(2,1)} %param.13, f32[2,8,121]{2,0,1:T(2,128)S(1)} %fusion.5), kind=kOutput, calls=%fused_computation.21 | convolution fusion | flops 88550704 | bytes 6281594 | tf_op jit(solution)/shard_map/dot_general | solution.py:92
  154.7 104.3 %while.14 = (s32[]{:T(128)}, f32[16,256]{1,0:T(8,128)S(1)}, s32[16,27]{0,1:T(8,128)S(1)}, f32[16,3,256]{2,0,1:T(8,128)S(1)}, f32[48,4,256]{2,1,0:T(4,128)S(1)}, /*index=5*/s32[]{:T(128)}, s32[]{:T(128)}) while((s32[]{:T(128)}, f32[16,256]{1,0:T(8,128)S(1)}, s32[16,27]{0,1:T(8,128)S(1)}, f32[16,3,256]{2,0,1:T(8,128)S(1)}, ...), condition=%wide.region_2.3_spmd.clone, body=%wide.region_0.2_spmd.clone.sunk | while | flops 13706307 | bytes 807467 | solution.py:50
  155.5 3.0 %multiply_reduce_fusion.2 = f32[16,256]{1,0:T(8,128)S(1)} fusion(f32[16,256]{1,0:T(8,128)S(1)} %get-tuple-element.234, f32[16,256]{1,0:T(8,128)S(1)} %get-tuple-element.235, f32[16,256]{1,0:T(8,128)S(1)} %get-tuple-element.236, f32[16,256]{1,0:T(8,128)S(1)} %get-tuple-element.239, f32[16,256]{1,0:T(8,128)S(1)} %get-tuple-element.240, ...), kind=kLoop, calls=%fused_computation.5.clone.1 | loop fusion | flops 13627392 | bytes 196624 | tf_op jit(solution)/shard_map/while/body/eval_jaxpr/reduce_sum | solution.py:47
  159.3 3.0 %multiply_reduce_fusion.2 = f32[16,256]{1,0:T(8,128)S(1)} fusion(f32[16,256]{1,0:T(8,128)S(1)} %get-tuple-element.234, f32[16,256]{1,0:T(8,128)S(1)} %get-tuple-element.235, f32[16,256]{1,0:T(8,128)S(1)} %get-tuple-element.236, f32[16,256]{1,0:T(8,128)S(1)} %get-tuple-element.239, f32[16,256]{1,0:T(8,128)S(1)} %get-tuple-element.240, ...), kind=kLoop, calls=%fused_computation.5.clone.1 | loop fusion | flops 13627392 | bytes 196624 | tf_op jit(solution)/shard_map/while/body/eval_jaxpr/reduce_sum | solution.py:47
  163.2 3.0 %multiply_reduce_fusion.2 = f32[16,256]{1,0:T(8,128)S(1)} fusion(f32[16,256]{1,0:T(8,128)S(1)} %get-tuple-element.234, f32[16,256]{1,0:T(8,128)S(1)} %get-tuple-element.235, f32[16,256]{1,0:T(8,128)S(1)} %get-tuple-element.236, f32[16,256]{1,0:T(8,128)S(1)} %get-tuple-element.239, f32[16,256]{1,0:T(8,128)S(1)} %get-tuple-element.240, ...), kind=kLoop, calls=%fused_computation.5.clone.1 | loop fusion | flops 13627392 | bytes 196624 | tf_op jit(solution)/shard_map/while/body/eval_jaxpr/reduce_sum | solution.py:47
  167.1 3.0 %multiply_reduce_fusion.2 = f32[16,256]{1,0:T(8,128)S(1)} fusion(f32[16,256]{1,0:T(8,128)S(1)} %get-tuple-element.234, f32[16,256]{1,0:T(8,128)S(1)} %get-tuple-element.235, f32[16,256]{1,0:T(8,128)S(1)} %get-tuple-element.236, f32[16,256]{1,0:T(8,128)S(1)} %get-tuple-element.239, f32[16,256]{1,0:T(8,128)S(1)} %get-tuple-element.240, ...), kind=kLoop, calls=%fused_computation.5.clone.1 | loop fusion | flops 13627392 | bytes 196624 | tf_op jit(solution)/shard_map/while/body/eval_jaxpr/reduce_sum | solution.py:47
  170.9 3.0 %multiply_reduce_fusion.2 = f32[16,256]{1,0:T(8,128)S(1)} fusion(f32[16,256]{1,0:T(8,128)S(1)} %get-tuple-element.234, f32[16,256]{1,0:T(8,128)S(1)} %get-tuple-element.235, f32[16,256]{1,0:T(8,128)S(1)} %get-tuple-element.236, f32[16,256]{1,0:T(8,128)S(1)} %get-tuple-element.239, f32[16,256]{1,0:T(8,128)S(1)} %get-tuple-element.240, ...), kind=kLoop, calls=%fused_computation.5.clone.1 | loop fusion | flops 13627392 | bytes 196624 | tf_op jit(solution)/shard_map/while/body/eval_jaxpr/reduce_sum | solution.py:47
  174.8 3.0 %multiply_reduce_fusion.2 = f32[16,256]{1,0:T(8,128)S(1)} fusion(f32[16,256]{1,0:T(8,128)S(1)} %get-tuple-element.234, f32[16,256]{1,0:T(8,128)S(1)} %get-tuple-element.235, f32[16,256]{1,0:T(8,128)S(1)} %get-tuple-element.236, f32[16,256]{1,0:T(8,128)S(1)} %get-tuple-element.239, f32[16,256]{1,0:T(8,128)S(1)} %get-tuple-element.240, ...), kind=kLoop, calls=%fused_computation.5.clone.1 | loop fusion | flops 13627392 | bytes 196624 | tf_op jit(solution)/shard_map/while/body/eval_jaxpr/reduce_sum | solution.py:47
  178.7 3.0 %multiply_reduce_fusion.2 = f32[16,256]{1,0:T(8,128)S(1)} fusion(f32[16,256]{1,0:T(8,128)S(1)} %get-tuple-element.234, f32[16,256]{1,0:T(8,128)S(1)} %get-tuple-element.235, f32[16,256]{1,0:T(8,128)S(1)} %get-tuple-element.236, f32[16,256]{1,0:T(8,128)S(1)} %get-tuple-element.239, f32[16,256]{1,0:T(8,128)S(1)} %get-tuple-element.240, ...), kind=kLoop, calls=%fused_computation.5.clone.1 | loop fusion | flops 13627392 | bytes 196624 | tf_op jit(solution)/shard_map/while/body/eval_jaxpr/reduce_sum | solution.py:47
  186.4 3.0 %multiply_reduce_fusion.2 = f32[16,256]{1,0:T(8,128)S(1)} fusion(f32[16,256]{1,0:T(8,128)S(1)} %get-tuple-element.234, f32[16,256]{1,0:T(8,128)S(1)} %get-tuple-element.235, f32[16,256]{1,0:T(8,128)S(1)} %get-tuple-element.236, f32[16,256]{1,0:T(8,128)S(1)} %get-tuple-element.239, f32[16,256]{1,0:T(8,128)S(1)} %get-tuple-element.240, ...), kind=kLoop, calls=%fused_computation.5.clone.1 | loop fusion | flops 13627392 | bytes 196624 | tf_op jit(solution)/shard_map/while/body/eval_jaxpr/reduce_sum | solution.py:47
  194.1 3.0 %multiply_reduce_fusion.2 = f32[16,256]{1,0:T(8,128)S(1)} fusion(f32[16,256]{1,0:T(8,128)S(1)} %get-tuple-element.234, f32[16,256]{1,0:T(8,128)S(1)} %get-tuple-element.235, f32[16,256]{1,0:T(8,128)S(1)} %get-tuple-element.236, f32[16,256]{1,0:T(8,128)S(1)} %get-tuple-element.239, f32[16,256]{1,0:T(8,128)S(1)} %get-tuple-element.240, ...), kind=kLoop, calls=%fused_computation.5.clone.1 | loop fusion | flops 13627392 | bytes 196624 | tf_op jit(solution)/shard_map/while/body/eval_jaxpr/reduce_sum | solution.py:47
  209.6 3.0 %multiply_reduce_fusion.2 = f32[16,256]{1,0:T(8,128)S(1)} fusion(f32[16,256]{1,0:T(8,128)S(1)} %get-tuple-element.234, f32[16,256]{1,0:T(8,128)S(1)} %get-tuple-element.235, f32[16,256]{1,0:T(8,128)S(1)} %get-tuple-element.236, f32[16,256]{1,0:T(8,128)S(1)} %get-tuple-element.239, f32[16,256]{1,0:T(8,128)S(1)} %get-tuple-element.240, ...), kind=kLoop, calls=%fused_computation.5.clone.1 | loop fusion | flops 13627392 | bytes 196624 | tf_op jit(solution)/shard_map/while/body/eval_jaxpr/reduce_sum | solution.py:47
  213.4 3.0 %multiply_reduce_fusion.2 = f32[16,256]{1,0:T(8,128)S(1)} fusion(f32[16,256]{1,0:T(8,128)S(1)} %get-tuple-element.234, f32[16,256]{1,0:T(8,128)S(1)} %get-tuple-element.235, f32[16,256]{1,0:T(8,128)S(1)} %get-tuple-element.236, f32[16,256]{1,0:T(8,128)S(1)} %get-tuple-element.239, f32[16,256]{1,0:T(8,128)S(1)} %get-tuple-element.240, ...), kind=kLoop, calls=%fused_computation.5.clone.1 | loop fusion | flops 13627392 | bytes 196624 | tf_op jit(solution)/shard_map/while/body/eval_jaxpr/reduce_sum | solution.py:47
  228.9 3.0 %multiply_reduce_fusion.2 = f32[16,256]{1,0:T(8,128)S(1)} fusion(f32[16,256]{1,0:T(8,128)S(1)} %get-tuple-element.234, f32[16,256]{1,0:T(8,128)S(1)} %get-tuple-element.235, f32[16,256]{1,0:T(8,128)S(1)} %get-tuple-element.236, f32[16,256]{1,0:T(8,128)S(1)} %get-tuple-element.239, f32[16,256]{1,0:T(8,128)S(1)} %get-tuple-element.240, ...), kind=kLoop, calls=%fused_computation.5.clone.1 | loop fusion | flops 13627392 | bytes 196624 | tf_op jit(solution)/shard_map/while/body/eval_jaxpr/reduce_sum | solution.py:47
  232.7 3.0 %multiply_reduce_fusion.2 = f32[16,256]{1,0:T(8,128)S(1)} fusion(f32[16,256]{1,0:T(8,128)S(1)} %get-tuple-element.234, f32[16,256]{1,0:T(8,128)S(1)} %get-tuple-element.235, f32[16,256]{1,0:T(8,128)S(1)} %get-tuple-element.236, f32[16,256]{1,0:T(8,128)S(1)} %get-tuple-element.239, f32[16,256]{1,0:T(8,128)S(1)} %get-tuple-element.240, ...), kind=kLoop, calls=%fused_computation.5.clone.1 | loop fusion | flops 13627392 | bytes 196624 | tf_op jit(solution)/shard_map/while/body/eval_jaxpr/reduce_sum | solution.py:47
  240.5 3.0 %multiply_reduce_fusion.2 = f32[16,256]{1,0:T(8,128)S(1)} fusion(f32[16,256]{1,0:T(8,128)S(1)} %get-tuple-element.234, f32[16,256]{1,0:T(8,128)S(1)} %get-tuple-element.235, f32[16,256]{1,0:T(8,128)S(1)} %get-tuple-element.236, f32[16,256]{1,0:T(8,128)S(1)} %get-tuple-element.239, f32[16,256]{1,0:T(8,128)S(1)} %get-tuple-element.240, ...), kind=kLoop, calls=%fused_computation.5.clone.1 | loop fusion | flops 13627392 | bytes 196624 | tf_op jit(solution)/shard_map/while/body/eval_jaxpr/reduce_sum | solution.py:47
  244.3 3.0 %multiply_reduce_fusion.2 = f32[16,256]{1,0:T(8,128)S(1)} fusion(f32[16,256]{1,0:T(8,128)S(1)} %get-tuple-element.234, f32[16,256]{1,0:T(8,128)S(1)} %get-tuple-element.235, f32[16,256]{1,0:T(8,128)S(1)} %get-tuple-element.236, f32[16,256]{1,0:T(8,128)S(1)} %get-tuple-element.239, f32[16,256]{1,0:T(8,128)S(1)} %get-tuple-element.240, ...), kind=kLoop, calls=%fused_computation.5.clone.1 | loop fusion | flops 13627392 | bytes 196624 | tf_op jit(solution)/shard_map/while/body/eval_jaxpr/reduce_sum | solution.py:47
  248.2 3.0 %multiply_reduce_fusion.2 = f32[16,256]{1,0:T(8,128)S(1)} fusion(f32[16,256]{1,0:T(8,128)S(1)} %get-tuple-element.234, f32[16,256]{1,0:T(8,128)S(1)} %get-tuple-element.235, f32[16,256]{1,0:T(8,128)S(1)} %get-tuple-element.236, f32[16,256]{1,0:T(8,128)S(1)} %get-tuple-element.239, f32[16,256]{1,0:T(8,128)S(1)} %get-tuple-element.240, ...), kind=kLoop, calls=%fused_computation.5.clone.1 | loop fusion | flops 13627392 | bytes 196624 | tf_op jit(solution)/shard_map/while/body/eval_jaxpr/reduce_sum | solution.py:47
  252.0 3.0 %multiply_reduce_fusion.2 = f32[16,256]{1,0:T(8,128)S(1)} fusion(f32[16,256]{1,0:T(8,128)S(1)} %get-tuple-element.234, f32[16,256]{1,0:T(8,128)S(1)} %get-tuple-element.235, f32[16,256]{1,0:T(8,128)S(1)} %get-tuple-element.236, f32[16,256]{1,0:T(8,128)S(1)} %get-tuple-element.239, f32[16,256]{1,0:T(8,128)S(1)} %get-tuple-element.240, ...), kind=kLoop, calls=%fused_computation.5.clone.1 | loop fusion | flops 13627392 | bytes 196624 | tf_op jit(solution)/shard_map/while/body/eval_jaxpr/reduce_sum | solution.py:47
  (340 shorter events, 62.1 us)
Async XLA Ops:
  0.6 40.9 %copy-start = (f32[8,121,121]{2,0,1:T(8,128)S(1)}, f32[8,121,121]{2,0,1:T(8,128)}, u32[]{:S(2)}) copy-start(f32[8,121,121]{2,0,1:T(8,128)} %param.15) | copy-start | bytes 1405540
  2.4 152.2 %collective-permute-start.1 = (f32[16,4,256]{2,1,0:T(4,128)S(1)}, f32[16,4,256]{2,1,0:T(4,128)S(1)}, u32[]{:S(2)}, u32[]{:S(2)}) collective-permute-start(f32[16,4,256]{2,1,0:T(4,128)S(1)} %pad_maximum_fusion.1), channel_id=1, source_target_pairs={{1,0},{2,1},{3,2},{4,3},{5,4},{6,5},{7,6},{8,7},{9,8},{10,9},{11,1... | collective-permute-start | bytes 196616 | tf_op jit(solution)/shard_map/ppermute | solution.py:19
  3.7 150.9 %collective-permute-start = (f32[16,4,256]{2,1,0:T(4,128)S(1)}, f32[16,4,256]{2,1,0:T(4,128)S(1)}, u32[]{:S(2)}, u32[]{:S(2)}) collective-permute-start(f32[16,4,256]{2,1,0:T(4,128)S(1)} %pad_maximum_fusion.1), channel_id=1, source_target_pairs={{0,1},{1,2},{2,3},{3,4},{4,5},{5,6},{6,7},{7,8},{8,9},{9,10},{10,1... | collective-permute-start | bytes 196616 | tf_op jit(solution)/shard_map/ppermute | solution.py:17
  9.8 91.7 %all-to-all-start = ((s32[64,1,4]{2,1,0:T(1,128)}), s32[64,1,4]{2,1,0:T(1,128)S(1)}, u32[]{:S(2)}, u32[]{:S(2)}) async-start(s32[64,1,4]{2,1,0:T(1,128)} %bitcast), calls=%async_computation | async-start | bytes 65536 | tf_op jit(solution)/shard_map/all_to_all | solution.py:79
  101.5 37.6 %copy-start.2 = (s32[16,189]{1,0:T(8,128)S(1)}, s32[16,189]{1,0:T(8,128)}, u32[]{:S(2)}) copy-start(s32[16,189]{1,0:T(8,128)} %param.17) | copy-start | bytes 36292
  149.4 5.2 %copy-start.1 = (f32[16,3,256]{2,0,1:T(8,128)S(1)}, f32[16,3,256]{2,0,1:T(8,128)}, u32[]{:S(2)}) copy-start(f32[16,3,256]{2,0,1:T(8,128)} %param.18) | copy-start | bytes 147460
  154.7 104.3 %copy-start.3 = (s32[16]{0:T(128)S(1)}, s32[16]{0:T(128)}, u32[]{:S(2)}) copy-start(s32[16]{0:T(128)} %param.20) | copy-start | bytes 196
where the time goes:
time: 261 us; the launch traced here: 260 us
  other arithmetic  88.2 us (34%)
  local copies, waits for them, and re-layouts  69.1 us (26%)
  blocking collectives  57.9 us (22%)
  starting transfers between devices  36.2 us (14%)
  matrix products  5.34 us (2%)
    reduce_sum x27, other arithmetic, one_member(): partial_sum = jnp.sum(kernel * sources[:, 3, None, :], axis=2)  80.5 us
    all_gather x1, blocking collectives, per_device(): everything = lax.all_gather(multipoles, 'zone', axis=0, tiled=True)  57.9 us
    gather x2, local copies, waits for them, and re-layouts, per_device(): remote_box = slot_boxes[peer_zone, slot_index]  37.6 us
    all_to_all x1, starting transfers between devices, per_device(): lax.all_to_all(outgoing, 'zone', split_axis=0, concat_axis=0, tiled=True)  30.3 us
    gather x27, local copies, waits for them, and re-layouts, one_member(): sources = window[jnp.maximum(list_entry, 0)]  16 us
    gather x2, local copies, waits for them, and re-layouts, per_device(): gathered = everything[row_index]  9.53 us
  transfers between devices with their start and end apart: 3, of which 0 were waited for; matrix products, arithmetic and copies ran while one was open for 22% of the time, Pallas kernels for 0%

commit v1 on v0

v1 whole, which is shorter than its diff:
```python
import jax
import jax.numpy as jnp
from jax import lax
from jax.experimental import pallas as pl
from jax.experimental.pallas import tpu as pltpu
from jax.sharding import PartitionSpec as P

soften = 0.0025
BOX = 16
S = 256
HALF = 128
FEATURES = 32
NEAR = 27
WINDOW = 48
OFFSETS = 189
P2 = 121
GROUP = 8
ROWS = 32
TABLE = 384
MESH = pl.DeviceIdType.MESH
F32 = jnp.float32
BF16 = jnp.bfloat16


def iota(shape, dim):
    return lax.broadcasted_iota(jnp.int32, shape, dim)


def flag(mask, kind=BF16):
    return jnp.where(mask, 1.0, 0.0).astype(kind)


def dot(a, b):
    return jnp.dot(a, b, preferred_element_type=F32)


def dot_t(a, b):
    return lax.dot_general(a, b, (((1,), (1,)), ((), ())), preferred_element_type=F32)


def code(across, along):
    return across % 2 + 4 * (across // 2) + 2 * (along % 2) + 8 * (along // 2)


def split(x):
    high = x.astype(BF16).astype(F32)
    rest = x - high
    middle = rest.astype(BF16).astype(F32)
    return high, middle, rest - middle


def write_features(ref, coordinates, target):
    parts = [split(u) for u in coordinates]
    norm = coordinates[0] * coordinates[0]
    for u in coordinates[1:]:
        norm = norm + u * u
    ones = jnp.ones_like(norm)
    zeros = jnp.zeros_like(norm)
    rows = []
    for high, middle, low in parts:
        if target:
            rows += [-2.0 * r for r in (high, high, middle, middle, high, low)]
        else:
            rows += [high, middle, high, middle, low, high]
    if target:
        rows += list(split(norm)) + [ones] * 3
    else:
        rows += [ones] * 3 + list(split(norm + soften))
    rows += [zeros] * (FEATURES - len(rows))
    for k, row in enumerate(rows):
        ref[:, k, :] = row


def kernel(
    multipoles,
    operators_hbm,
    parents,
    shifts_hbm,
    slots,
    lists,
    positions,
    charges,
    counts,
    near,
    local_out,
    potential_out,
    ops,
    shifts,
    halo_out,
    halo_in,
    back_out,
    back_in,
    chosen,
    relay,
    onward,
    table,
    features,
    sources,
    above,
    targets,
    charge_columns,
    present,
    sums,
    own_sums,
    above_sums,
    gathered,
    parent_columns,
    load_sem,
    halo_sem,
    back_sem,
    first_send,
    first_recv,
    second_send,
    second_recv,
):
    zone = lax.axis_index("zone")
    level = lax.axis_index("level")
    levels = lax.axis_size("level")
    place = zone % GROUP
    group = zone // GROUP

    def first_peer(d):
        return (group * GROUP + (place + d) % GROUP, level)

    def second_peer(d):
        return (((group + d) % GROUP) * GROUP + place, level)

    up = (zone, (level + 1) % levels)
    down = (zone, (level + levels - 1) % levels)

    barrier = pltpu.get_barrier_semaphore()
    for peer in [down, up] + [first_peer(d) for d in range(1, GROUP)] + [
        second_peer(d) for d in range(1, GROUP)
    ]:
        pl.semaphore_signal(barrier, inc=1, device_id=peer, device_id_type=MESH)

    load_ops = pltpu.make_async_copy(operators_hbm, ops, load_sem.at[0])
    load_ops.start()
    load_shifts = pltpu.make_async_copy(shifts_hbm, shifts, load_sem.at[1])
    load_shifts.start()

    diagonal = iota((BOX, BOX), 0) == iota((BOX, BOX), 1)
    count_row = counts[...].reshape(1, BOX).astype(F32)
    count_column = jnp.sum(jnp.where(diagonal, count_row, 0.0), axis=1, keepdims=True)
    occupied = iota((BOX, S), 1).astype(F32) < count_column
    for c in range(3):
        x = positions[c]
        halo_out[c] = jnp.where(occupied, x, x[:, 0:1])
    halo_out[3] = jnp.where(occupied, charges[...], 0.0)

    own = jnp.concatenate(
        [multipoles[...], jnp.zeros((BOX, HALF - P2), BF16)], axis=1
    )
    r = iota((S, 64), 0)
    reader = (r // 4) % GROUP * GROUP + r // ROWS
    slot_rows = dot_t(flag(reader == iota((S, 64), 1)), slots[0].astype(F32).astype(BF16))
    mine = iota((S, 4), 0) % 4 == iota((S, 4), 1)
    picked = jnp.where(mine, slot_rows, 0.0).astype(BF16)
    box_of = dot(picked, jnp.ones((4, BOX), BF16))
    one_hot = flag(box_of == iota((S, BOX), 1).astype(F32))
    chosen[...] = dot(one_hot, own).astype(BF16).reshape(GROUP, ROWS, HALF)

    pl.semaphore_wait(barrier, 2 * GROUP)

    halo_copy = pltpu.make_async_remote_copy(
        src_ref=halo_out,
        dst_ref=halo_in,
        send_sem=halo_sem.at[0],
        recv_sem=halo_sem.at[1],
        device_id=down,
        device_id_type=MESH,
    )
    back_copy = pltpu.make_async_remote_copy(
        src_ref=back_out,
        dst_ref=back_in,
        send_sem=back_sem.at[0],
        recv_sem=back_sem.at[1],
        device_id=up,
        device_id_type=MESH,
    )

    @pl.when(level > 0)
    def _():
        halo_copy.start()

    def first_copy(d, slot):
        return pltpu.make_async_remote_copy(
            src_ref=chosen.at[(place + d) % GROUP],
            dst_ref=relay.at[slot],
            send_sem=first_send.at[d - 1],
            recv_sem=first_recv.at[d - 1],
            device_id=first_peer(d),
            device_id_type=MESH,
        )

    def second_copy(d, slot):
        return pltpu.make_async_remote_copy(
            src_ref=onward.at[(group + d) % GROUP],
            dst_ref=table.at[slot],
            send_sem=second_send.at[d - 1],
            recv_sem=second_recv.at[d - 1],
            device_id=second_peer(d),
            device_id_type=MESH,
        )

    for d in range(1, GROUP):
        first_copy(d, place).start()
    relay[place] = chosen[place]

    middle = [jnp.sum(halo_out[c, :, 0:1], axis=0, keepdims=True) * (1.0 / BOX) for c in range(3)]
    offsets = [halo_out[c] - middle[c] for c in range(3)]
    identity = flag(iota((S, S), 0) == iota((S, S), 1))
    write_features(features, offsets, True)

    def prepare(b, carry):
        targets[b] = dot_t(identity, features[b].astype(BF16)).astype(BF16)
        row = jnp.broadcast_to(halo_out[3, pl.ds(b, 1), :], (HALF, S))
        charge_columns[b] = row.T
        sums[b] = jnp.zeros((S, HALF), F32)
        return carry

    lax.fori_loop(0, BOX, prepare, 0)
    write_features(features, offsets, False)
    sources[...] = features[...].astype(BF16)
    own_sums[...] = jnp.zeros_like(own_sums)
    above_sums[...] = jnp.zeros_like(above_sums)
    hits = flag(near[...][:, None, :] == iota((BOX, WINDOW, NEAR), 1))
    present[...] = dot(
        hits.reshape(BOX * WINDOW, NEAR), jnp.ones((NEAR, HALF), BF16)
    ).reshape(BOX, WINDOW, HALF)

    def block(b, n, shift, side, charge, other):
        y = lax.rsqrt(dot(targets[b], side[n]))
        if other is None:
            y = jnp.where(iota((S, S), 0) == iota((S, S), 1), 0.0, y)
        there = present[b, pl.ds(shift + n, 1), :]
        row = charge[3, pl.ds(n, 1), :]
        left, right = y[:, :HALF], y[:, HALF:]
        sums[b] = sums[b] + (left * (row[:, :HALF] * there) + right * (row[:, HALF:] * there))
        if other is not None:
            column = charge_columns[b]
            for half, part in ((0, left), (HALF, right)):
                total = (part * column).reshape(S // 8, 8, HALF).sum(0)
                other[n, :, half : half + HALF] = (
                    other[n, :, half : half + HALF] + total * there
                )

    def own_block(b, n):
        block(b, n, BOX, sources, halo_out, own_sums)

    def own_pairs(s, carry):
        for w in range(4):
            own_block(code(s, w), code(s + 1, w))
            own_block(code(w, s), code(w, s + 1))
        for w in range(3):
            own_block(code(s, w), code(s + 1, w + 1))
            own_block(code(s + 1, w), code(s, w + 1))
        return carry

    def self_pairs(s, carry):
        for w in range(4):
            block(4 * s + w, 4 * s + w, BOX, sources, halo_out, None)
        return carry

    lax.fori_loop(0, 3, own_pairs, 0)

    for d in range(1, GROUP):
        first_copy(d, (place + GROUP - d) % GROUP).wait_recv()
    r0 = iota((S, S), 0)
    wanted = (r0 // 4) % GROUP * ROWS + r0 // ROWS * 4 + r0 % 4
    order = flag(wanted == iota((S, S), 1))
    onward[...] = (
        dot(order, relay[...].reshape(S, HALF)).astype(BF16).reshape(GROUP, ROWS, HALF)
    )
    for d in range(1, GROUP):
        second_copy(d, group).start()
    table[group] = onward[group]

    @pl.when(level < levels - 1)
    def _():
        halo_copy.wait_recv()
        write_features(features, [halo_in[c] - middle[c] for c in range(3)], False)
        above[...] = features[...].astype(BF16)

        def above_pairs(t, carry):
            x = (t + 1) // 3
            x_next = t - 2 * x
            for w in range(10):
                y = (w + 1) // 3
                y_next = w - 2 * y
                block(code(x, y), code(x_next, y_next), 2 * BOX, above, halo_in, above_sums)
            return carry

        lax.fori_loop(0, 10, above_pairs, 0)
        back_out[...] = jnp.sum(above_sums[...], axis=1)
        back_copy.start()

    lax.fori_loop(0, 4, self_pairs, 0)

    for d in range(1, GROUP):
        second_copy(d, (group + GROUP - d) % GROUP).wait_recv()
    whole = jnp.concatenate(
        [own, table[...].reshape(S, HALF), jnp.zeros((TABLE - S - BOX, HALF), BF16)], axis=0
    )
    columns = whole.T
    box_row = iota((TABLE, OFFSETS), 0)
    for b in range(BOX):
        named = flag(box_row == lists[b : b + 1, :])
        gathered[:, b, :] = dot(columns, named)

    load_ops.wait()

    def translate(s, total):
        for w in range(11):
            p = s * 11 + w
            total = total + dot(gathered[p].astype(BF16), ops[p])
        return total

    far = lax.fori_loop(0, P2 // 11, translate, jnp.zeros((BOX, P2), F32))

    load_shifts.wait()
    for g in range(2):
        row = jnp.concatenate([parents[g : g + 1, :], jnp.zeros((1, HALF - P2), F32)], axis=1)
        parent_columns[g] = jnp.broadcast_to(row, (HALF, HALF)).T
    downward = []
    for g in range(2):
        total = jnp.zeros((8, P2), F32)
        for p in range(P2):
            total = total + parent_columns[g, p : p + 1, :P2] * shifts[p]
        downward.append(total)
    local_out[...] = far + jnp.concatenate(downward, axis=0)

    def finish(b, carry):
        mine = jnp.sum(sums[b].T, axis=0, keepdims=True)
        theirs = jnp.sum(own_sums[b], axis=0, keepdims=True)
        potential_out[pl.ds(b, 1), :] = mine + theirs
        return carry

    lax.fori_loop(0, BOX, finish, 0)

    @pl.when(level > 0)
    def _():
        back_copy.wait_recv()
        potential_out[...] = potential_out[...] + back_in[...]
        halo_copy.wait_send()

    @pl.when(level < levels - 1)
    def _():
        back_copy.wait_send()

    potential_out[...] = jnp.where(occupied, potential_out[...], 0.0)
    for d in range(1, GROUP):
        first_copy(d, place).wait_send()
        second_copy(d, group).wait_send()


def per_device(
    multipoles,
    operators,
    parent_locals,
    shifts,
    send_slots,
    lists,
    positions,
    charges,
    counts,
    near_lists,
):
    arguments = (
        multipoles,
        operators.transpose(1, 0, 2),
        parent_locals,
        shifts.transpose(1, 0, 2),
        send_slots.transpose(0, 2, 1),
        lists,
        positions.transpose(1, 0, 2),
        charges,
        counts,
        near_lists,
    )
    vmem = pl.BlockSpec(memory_space=pltpu.VMEM)
    anywhere = pl.BlockSpec(memory_space=pl.ANY)
    specs = [vmem, anywhere, vmem, anywhere, vmem, vmem, vmem, vmem, vmem, vmem]
    return pl.pallas_call(
        kernel,
        out_shape=(
            jax.ShapeDtypeStruct((BOX, P2), F32),
            jax.ShapeDtypeStruct((BOX, S), F32),
        ),
        in_specs=specs,
        out_specs=(vmem, vmem),
        scratch_shapes=[
            pltpu.VMEM((P2, OFFSETS, P2), BF16),
            pltpu.VMEM((P2, 8, P2), F32),
            pltpu.VMEM((4, BOX, S), F32),
            pltpu.VMEM((4, BOX, S), F32),
            pltpu.VMEM((BOX, S), F32),
            pltpu.VMEM((BOX, S), F32),
            pltpu.VMEM((GROUP, ROWS, HALF), BF16),
            pltpu.VMEM((GROUP, ROWS, HALF), BF16),
            pltpu.VMEM((GROUP, ROWS, HALF), BF16),
            pltpu.VMEM((GROUP, ROWS, HALF), BF16),
            pltpu.VMEM((BOX, FEATURES, S), F32),
            pltpu.VMEM((BOX, FEATURES, S), BF16),
            pltpu.VMEM((BOX, FEATURES, S), BF16),
            pltpu.VMEM((BOX, S, FEATURES), BF16),
            pltpu.VMEM((BOX, S, HALF), F32),
            pltpu.VMEM((BOX, WINDOW, HALF), F32),
            pltpu.VMEM((BOX, S, HALF), F32),
            pltpu.VMEM((BOX, 8, S), F32),
            pltpu.VMEM((BOX, 8, S), F32),
            pltpu.VMEM((HALF, BOX, OFFSETS), F32),
            pltpu.VMEM((2, HALF, HALF), F32),
            pltpu.SemaphoreType.DMA((2,)),
            pltpu.SemaphoreType.DMA((2,)),
            pltpu.SemaphoreType.DMA((2,)),
            pltpu.SemaphoreType.DMA((GROUP - 1,)),
            pltpu.SemaphoreType.DMA((GROUP - 1,)),
            pltpu.SemaphoreType.DMA((GROUP - 1,)),
            pltpu.SemaphoreType.DMA((GROUP - 1,)),
        ],
        compiler_params=pltpu.CompilerParams(
            collective_id=0, has_side_effects=True, vmem_limit_bytes=48 * 2**20
        ),
    )(*arguments)


def solution(mesh):
    placed = (
        P(("zone", "level"), None),
        P(),
        P(("zone", "level"), None),
        P(),
        P(("zone", "level"), None, None),
        P(("zone", "level"), None),
        P(("zone", "level"), None, None),
        P(("zone", "level"), None),
        P(("zone", "level")),
        P(("zone", "level"), None),
    )
    return jax.shard_map(
        per_device,
        mesh=mesh,
        in_specs=placed,
        out_specs=(P(("zone", "level"), None), P(("zone", "level"), None)),
        check_vma=False,
    )
```

time: 261 us -> 60.9 us (0.23)
  the two profiles are of different devices: /device:TPU:1 before, /device:TPU:16 now
where the time goes in v1:
time: 60.9 us; the launch traced here: 60.4 us
  Pallas kernels  51.9 us (85%)
  local copies, waits for them, and re-layouts  7.86 us (13%)
  between operations  0.66 us (1%)
    pallas_call x1, Pallas kernels, per_device(): pl.pallas_call(kernel, out_shape=(jax.ShapeDtypeStruct((BOX, P2), F32), j...  51.9 us
    unnamed x20, local copies, waits for them, and re-layouts  7.86 us

profile of v1, /device:TPU:16, one launch (start us, length us, event | category | flops | bytes accessed | tf_op | source)
XLA Modules:
  0.0 60.4 jit_solution(12421709845115376260)
XLA Ops:
  0.6 0.0 copy-start
  0.6 1.0 %copy-done = f32[8,121,121]{2,0,1:T(8,128)S(1)} copy-done((f32[8,121,121]{2,0,1:T(8,128)S(1)}, f32[8,121,121]{2,0,1:T(8,128)}, u32[]{:S(2)}) %copy-start) | copy-done | bytes 468536
  1.7 0.0 copy-start.1
  1.7 0.8 %copy-done.1 = f32[16,3,256]{2,0,1:T(8,128)S(1)} copy-done((f32[16,3,256]{2,0,1:T(8,128)S(1)}, f32[16,3,256]{2,0,1:T(8,128)}, u32[]{:S(2)}) %copy-start.1) | copy-done | bytes 49176
  2.5 0.0 copy-start.2
  2.5 0.7 %copy-done.2 = s32[16,189]{1,0:T(8,128)S(1)} copy-done((s32[16,189]{1,0:T(8,128)S(1)}, s32[16,189]{1,0:T(8,128)}, u32[]{:S(2)}) %copy-start.2) | copy-done | bytes 12120
  3.2 0.0 copy-start.3
  3.2 0.7 %copy-done.3 = f32[16,256]{1,0:T(8,128)S(1)} copy-done((f32[16,256]{1,0:T(8,128)S(1)}, f32[16,256]{1,0:T(8,128)}, u32[]{:S(2)}) %copy-start.3) | copy-done | bytes 16408
  3.9 0.0 copy-start.4
  3.9 0.7 %copy-done.4 = s32[16,27]{1,0:T(8,128)S(1)} copy-done((s32[16,27]{1,0:T(8,128)S(1)}, s32[16,27]{1,0:T(8,128)}, u32[]{:S(2)}) %copy-start.4) | copy-done | bytes 1752
  4.6 0.0 copy-start.5
  4.6 0.7 %copy-done.5 = bf16[16,121]{1,0:T(8,128)(2,1)S(1)} copy-done((bf16[16,121]{1,0:T(8,128)(2,1)S(1)}, bf16[16,121]{1,0:T(8,128)(2,1)}, u32[]{:S(2)}) %copy-start.5) | copy-done | bytes 3896
  5.3 0.0 copy-start.6
  5.3 0.7 %copy-done.6 = s32[1,64,4]{1,2,0:T(4,128)S(1)} copy-done((s32[1,64,4]{1,2,0:T(4,128)S(1)}, s32[1,64,4]{1,2,0:T(4,128)}, u32[]{:S(2)}) %copy-start.6) | copy-done | bytes 1048
  6.0 0.0 copy-start.7
  6.0 0.7 %copy-done.7 = f32[2,121]{1,0:T(2,128)S(1)} copy-done((f32[2,121]{1,0:T(2,128)S(1)}, f32[2,121]{1,0:T(2,128)}, u32[]{:S(2)}) %copy-start.7) | copy-done | bytes 992
  6.6 0.0 copy-start.8
  6.6 0.7 %copy-done.8 = s32[16]{0:T(128)S(1)} copy-done((s32[16]{0:T(128)S(1)}, s32[16]{0:T(128)}, u32[]{:S(2)}) %copy-start.8) | copy-done | bytes 88
  7.3 51.9 %shard_map.113 = (f32[16,121]{1,0:T(8,128)S(1)}, f32[16,256]{1,0:T(8,128)S(1)}) custom-call(bf16[16,121]{1,0:T(8,128)(2,1)S(1)} %copy-done.5, bf16[121,189,121]{2,1,0:T(8,128)(2,1)} %bitcast.7, f32[2,121]{1,0:T(2,128)S(1)} %copy-done.7, f32[121,8,121]{2,1,0:T(8,128)S(1)} %bitcast.4, s32[1,4,64]{2,1,0:T(4,128)S(1)} %bitcast.6, s32[16,189]{1,0:T(8,128)S(1)} %copy-done.2, ...), custom_call_target="tpu_custom_call" | custom-call | tf_op jit(solution)/shard_map/pallas_call | solution.py:384
  59.2 0.6 copy.14
  59.8 0.6 %copy.15 = f32[16,256]{1,0:T(8,128)} copy(f32[16,256]{1,0:T(8,128)S(1)} %get-tuple-element.5) | data formatting | bytes 32768
Async XLA Ops:
  0.6 1.0 %copy-start = (f32[8,121,121]{2,0,1:T(8,128)S(1)}, f32[8,121,121]{2,0,1:T(8,128)}, u32[]{:S(2)}) copy-start(f32[8,121,121]{2,0,1:T(8,128)} %param.13) | copy-start | bytes 1405540
  1.7 0.8 %copy-start.1 = (f32[16,3,256]{2,0,1:T(8,128)S(1)}, f32[16,3,256]{2,0,1:T(8,128)}, u32[]{:S(2)}) copy-start(f32[16,3,256]{2,0,1:T(8,128)} %param.16) | copy-start | bytes 147460
  2.5 0.7 %copy-start.2 = (s32[16,189]{1,0:T(8,128)S(1)}, s32[16,189]{1,0:T(8,128)}, u32[]{:S(2)}) copy-start(s32[16,189]{1,0:T(8,128)} %lists.1) | copy-start | bytes 36292
  3.2 0.7 %copy-start.3 = (f32[16,256]{1,0:T(8,128)S(1)}, f32[16,256]{1,0:T(8,128)}, u32[]{:S(2)}) copy-start(f32[16,256]{1,0:T(8,128)} %charges.1) | copy-start | bytes 49156
  3.9 0.7 %copy-start.4 = (s32[16,27]{1,0:T(8,128)S(1)}, s32[16,27]{1,0:T(8,128)}, u32[]{:S(2)}) copy-start(s32[16,27]{1,0:T(8,128)} %near.1) | copy-start | bytes 5188
  4.6 0.7 %copy-start.5 = (bf16[16,121]{1,0:T(8,128)(2,1)S(1)}, bf16[16,121]{1,0:T(8,128)(2,1)}, u32[]{:S(2)}) copy-start(bf16[16,121]{1,0:T(8,128)(2,1)} %multipoles.1) | copy-start | bytes 11620
  5.3 0.7 %copy-start.6 = (s32[1,64,4]{1,2,0:T(4,128)S(1)}, s32[1,64,4]{1,2,0:T(4,128)}, u32[]{:S(2)}) copy-start(s32[1,64,4]{1,2,0:T(4,128)} %param.14) | copy-start | bytes 3076
  6.0 0.7 %copy-start.7 = (f32[2,121]{1,0:T(2,128)S(1)}, f32[2,121]{1,0:T(2,128)}, u32[]{:S(2)}) copy-start(f32[2,121]{1,0:T(2,128)} %parents.1) | copy-start | bytes 2908
  6.6 0.7 %copy-start.8 = (s32[16]{0:T(128)S(1)}, s32[16]{0:T(128)}, u32[]{:S(2)}) copy-start(s32[16]{0:T(128)} %counts.1) | copy-start | bytes 196

commit v2 on v1

v2 whole, which is shorter than its diff:
```python
import jax
import jax.numpy as jnp
from jax import lax
from jax.experimental import pallas as pl
from jax.experimental.pallas import tpu as pltpu
from jax.sharding import PartitionSpec as P

soften = 0.0025
BOX = 16
S = 256
HALF = 128
FEATURES = 32
NEAR = 27
WINDOW = 48
OFFSETS = 189
P2 = 121
DEPTH = 32
EXCEPTION = 45
MESH = pl.DeviceIdType.MESH
F32 = jnp.float32
BF16 = jnp.bfloat16


def iota(shape, dim):
    return lax.broadcasted_iota(jnp.int32, shape, dim)


def flag(mask, kind=BF16):
    return jnp.where(mask, 1.0, 0.0).astype(kind)


def dot(a, b):
    return jnp.dot(a, b, preferred_element_type=F32)


def dot_t(a, b):
    return lax.dot_general(a, b, (((1,), (1,)), ((), ())), preferred_element_type=F32)


def code(across, along):
    return across % 2 + 4 * (across // 2) + 2 * (along % 2) + 8 * (along // 2)


def split(x):
    high = x.astype(BF16).astype(F32)
    rest = x - high
    middle = rest.astype(BF16).astype(F32)
    return high, middle, rest - middle


def write_features(ref, coordinates, target):
    parts = [split(u) for u in coordinates]
    norm = coordinates[0] * coordinates[0]
    for u in coordinates[1:]:
        norm = norm + u * u
    ones = jnp.ones_like(norm)
    zeros = jnp.zeros_like(norm)
    rows = []
    for high, middle, low in parts:
        if target:
            rows += [-2.0 * r for r in (high, high, middle, middle, high, low)]
        else:
            rows += [high, middle, high, middle, low, high]
    if target:
        rows += list(split(norm)) + [ones] * 3
    else:
        rows += [ones] * 3 + list(split(norm + soften))
    rows += [zeros] * (FEATURES - len(rows))
    for k, row in enumerate(rows):
        ref[:, k, :] = row


def step(a, b):
    return (a + 64 - b) // 64


def first_level(level, levels):
    return (levels - 1 - level) // (levels - 1)


def zone_at(rank, level, levels):
    first = first_level(level, levels)
    at, after = step(rank, EXCEPTION), step(rank, EXCEPTION + 1)
    base = (rank + first * (1 - at)) * (1 - first * (at - after))
    distance = (base + 2) // 4
    side = ((base + 2) % 4) // 2
    z = (distance + side * (DEPTH - 2 * distance)) % DEPTH
    return 2 * z + base % 2


def rank_of(zone, level, levels):
    first = first_level(level, levels)
    z = zone // 2
    side = step(z, DEPTH // 2 + 1)
    distance = z + side * (DEPTH - 2 * z)
    base = 4 * distance - 2 + 2 * side + zone % 2 + 2 * (1 - step(z, 1))
    inside = step(base, 1)
    return base - first * (inside - step(base, EXCEPTION + 1)) + first * EXCEPTION * (1 - inside)


def kernel(
    multipoles_hbm,
    operators_hbm,
    parents_hbm,
    shifts_hbm,
    slots_hbm,
    lists_hbm,
    positions_hbm,
    charges_hbm,
    counts_hbm,
    near_hbm,
    local_out,
    potential_out,
    multipoles,
    ops,
    parents,
    shifts,
    slots,
    lists,
    positions,
    charges,
    counts,
    near,
    halo_out,
    halo_in,
    back_out,
    back_in,
    chosen,
    table,
    features,
    sources,
    below,
    targets,
    charge_columns,
    present,
    sums,
    own_sums,
    below_sums,
    named,
    gathered,
    parent_columns,
    load_sem,
    halo_sem,
    back_sem,
    slot_send,
    slot_recv,
):
    zone = lax.axis_index("zone")
    level = lax.axis_index("level")
    levels = lax.axis_size("level")
    zones = lax.axis_size("zone")
    rank = rank_of(zone, level, levels)

    loads = {}
    for k, (name, source, place) in enumerate(
        (
            ("multipoles", multipoles_hbm, multipoles),
            ("slots", slots_hbm, slots),
            ("counts", counts_hbm, counts),
            ("positions", positions_hbm, positions),
            ("charges", charges_hbm, charges),
            ("near", near_hbm, near),
            ("lists", lists_hbm, lists),
            ("parents", parents_hbm, parents),
            ("shifts", shifts_hbm, shifts),
            ("ops", operators_hbm, ops),
        )
    ):
        loads[name] = pltpu.make_async_copy(source, place, load_sem.at[k])
        loads[name].start()

    barrier = pltpu.get_barrier_semaphore()

    def tell(r, carry):
        pl.semaphore_signal(
            barrier, inc=1, device_id=(zone_at(r, level, levels), level), device_id_type=MESH
        )
        return carry

    lax.fori_loop(rank + 1, zones, tell, 0)

    @pl.when(level > 0)
    def _():
        pl.semaphore_signal(barrier, inc=1, device_id=(zone, level - 1), device_id_type=MESH)

    loads["multipoles"].wait()
    loads["slots"].wait()
    own = jnp.concatenate(
        [multipoles[...], jnp.zeros((BOX, HALF - P2), BF16)], axis=1
    )
    reader = iota((S, 64), 0) // 4
    slot_rows = dot_t(flag(reader == iota((S, 64), 1)), slots[0].astype(F32).astype(BF16))
    mine = iota((S, 4), 0) % 4 == iota((S, 4), 1)
    picked = jnp.where(mine, slot_rows, 0.0).astype(BF16)
    box_of = dot(picked, jnp.ones((4, BOX), BF16))
    one_hot = flag(box_of == iota((S, BOX), 1).astype(F32))
    chosen[...] = dot(one_hot, own).reshape(64, 4, HALF).astype(BF16)

    def slot_copy(source, place, peer):
        return pltpu.make_async_remote_copy(
            src_ref=chosen.at[source],
            dst_ref=table.at[place],
            send_sem=slot_send,
            recv_sem=slot_recv.at[place],
            device_id=(peer, level),
            device_id_type=MESH,
        )

    def send(r, carry):
        peer = zone_at(r, level, levels)
        slot_copy(peer, zone, peer).start()
        return carry

    def collect(r, carry):
        peer = zone_at(r, level, levels)
        slot_copy(peer, peer, peer).wait_recv()
        return carry

    def answer(r, carry):
        collect(r, carry)
        return send(r, carry)

    top = level // (levels - 1)

    @pl.when(rank + 1 - top > 0)
    def _():
        pl.semaphore_wait(barrier, rank + 1 - top)

    lax.fori_loop(0, rank, send, 0)
    table[zone] = chosen[zone]

    for name in ("counts", "positions", "charges"):
        loads[name].wait()
    diagonal = iota((BOX, BOX), 0) == iota((BOX, BOX), 1)
    count_row = counts[...].reshape(1, BOX).astype(F32)
    count_column = jnp.sum(jnp.where(diagonal, count_row, 0.0), axis=1, keepdims=True)
    occupied = iota((BOX, S), 1).astype(F32) < count_column
    for c in range(3):
        x = positions[c]
        halo_out[c] = jnp.where(occupied, x, x[:, 0:1])
    halo_out[3] = jnp.where(occupied, charges[...], 0.0)

    halo_copy = pltpu.make_async_remote_copy(
        src_ref=halo_out,
        dst_ref=halo_in,
        send_sem=halo_sem.at[0],
        recv_sem=halo_sem.at[1],
        device_id=(zone, (level + 1) % levels),
        device_id_type=MESH,
    )
    back_copy = pltpu.make_async_remote_copy(
        src_ref=back_out,
        dst_ref=back_in,
        send_sem=back_sem.at[0],
        recv_sem=back_sem.at[1],
        device_id=(zone, (level + levels - 1) % levels),
        device_id_type=MESH,
    )

    @pl.when(level < levels - 1)
    def _():
        halo_copy.start()

    middle = [jnp.sum(halo_out[c, :, 0:1], axis=0, keepdims=True) * (1.0 / BOX) for c in range(3)]
    offsets = [halo_out[c] - middle[c] for c in range(3)]
    identity = flag(iota((S, S), 0) == iota((S, S), 1))
    write_features(features, offsets, True)

    def prepare(b, carry):
        targets[b] = dot_t(identity, features[b].astype(BF16)).astype(BF16)
        row = jnp.broadcast_to(halo_out[3, pl.ds(b, 1), :], (HALF, S))
        charge_columns[b] = row.T
        sums[b] = jnp.zeros((S, HALF), F32)
        return carry

    lax.fori_loop(0, BOX, prepare, 0)
    write_features(features, offsets, False)
    sources[...] = features[...].astype(BF16)
    own_sums[...] = jnp.zeros_like(own_sums)
    below_sums[...] = jnp.zeros_like(below_sums)
    loads["near"].wait()
    hits = flag(near[...][:, None, :] == iota((BOX, WINDOW, NEAR), 1))
    present[...] = dot(
        hits.reshape(BOX * WINDOW, NEAR), jnp.ones((NEAR, HALF), BF16)
    ).reshape(BOX, WINDOW, HALF)

    def block(b, n, shift, side, charge, other):
        y = lax.rsqrt(dot(targets[b], side[n]))
        if other is None:
            y = jnp.where(iota((S, S), 0) == iota((S, S), 1), 0.0, y)
        there = present[b, pl.ds(shift + n, 1), :]
        row = charge[3, pl.ds(n, 1), :]
        left, right = y[:, :HALF], y[:, HALF:]
        sums[b] = sums[b] + (left * (row[:, :HALF] * there) + right * (row[:, HALF:] * there))
        if other is not None:
            column = charge_columns[b]
            for half, part in ((0, left), (HALF, right)):
                total = (part * column).reshape(S // 8, 8, HALF).sum(0)
                other[n, :, half : half + HALF] = (
                    other[n, :, half : half + HALF] + total * there
                )

    def own_block(b, n):
        block(b, n, BOX, sources, halo_out, own_sums)

    def own_pairs(s, carry):
        for w in range(4):
            own_block(code(s, w), code(s + 1, w))
            own_block(code(w, s), code(w, s + 1))
        for w in range(3):
            own_block(code(s, w), code(s + 1, w + 1))
            own_block(code(s + 1, w), code(s, w + 1))
        return carry

    def self_pairs(s, carry):
        for w in range(4):
            block(4 * s + w, 4 * s + w, BOX, sources, halo_out, None)
        return carry

    def below_pairs(t, carry):
        x = (t + 1) // 3
        x_next = t - 2 * x
        for w in range(10):
            y = (w + 1) // 3
            y_next = w - 2 * y
            block(code(x, y), code(x_next, y_next), 0, below, halo_in, below_sums)
        return carry

    lax.fori_loop(0, 3, own_pairs, 0)

    @pl.when(level > 0)
    def _():
        halo_copy.wait_recv()
        write_features(features, [halo_in[c] - middle[c] for c in range(3)], False)
        below[...] = features[...].astype(BF16)
        lax.fori_loop(0, 10, below_pairs, 0)
        back_out[...] = jnp.sum(below_sums[...], axis=1)
        back_copy.start()

    lax.fori_loop(0, 4, self_pairs, 0)

    loads["lists"].wait()
    own_columns = own.T
    for b in range(BOX):
        row = lists[b : b + 1, :]
        named[b] = flag(iota((S, OFFSETS), 0) + BOX == row)
        gathered[:, b, :] = dot(own_columns, flag(iota((BOX, OFFSETS), 0) == row))

    loads["parents"].wait()
    loads["shifts"].wait()
    for g in range(2):
        row = jnp.concatenate([parents[g : g + 1, :], jnp.zeros((1, HALF - P2), F32)], axis=1)
        parent_columns[g] = jnp.broadcast_to(row, (HALF, HALF)).T
    for g in range(2):
        total = jnp.zeros((8, P2), F32)
        for p in range(P2):
            total = total + parent_columns[g, p : p + 1, :P2] * shifts[p]
        local_out[8 * g : 8 * g + 8, :] = total

    def finish(b, carry):
        mine = jnp.sum(sums[b].T, axis=0, keepdims=True)
        theirs = jnp.sum(own_sums[b], axis=0, keepdims=True)
        potential_out[pl.ds(b, 1), :] = mine + theirs
        return carry

    lax.fori_loop(0, BOX, finish, 0)

    @pl.when(level < levels - 1)
    def _():
        back_copy.wait_recv()
        potential_out[...] = potential_out[...] + back_in[...]
        halo_copy.wait_send()

    @pl.when(level > 0)
    def _():
        back_copy.wait_send()

    potential_out[...] = jnp.where(occupied, potential_out[...], 0.0)
    loads["ops"].wait()

    lax.fori_loop(0, rank, collect, 0)
    lax.fori_loop(rank + 1, zones, answer, 0)
    columns = table[...].reshape(S, HALF).T
    for b in range(BOX):
        gathered[:, b, :] = gathered[:, b, :] + dot(columns, named[b])

    def translate(s, total):
        for w in range(11):
            p = s * 11 + w
            total = total + dot(gathered[p].astype(BF16), ops[p])
        return total

    far = lax.fori_loop(0, P2 // 11, translate, jnp.zeros((BOX, P2), F32), unroll=True)
    local_out[...] = local_out[...] + far
    pltpu.make_async_copy(chosen.at[pl.ds(1, 63)], chosen.at[pl.ds(1, 63)], slot_send).wait()


def per_device(
    multipoles,
    operators,
    parent_locals,
    shifts,
    send_slots,
    lists,
    positions,
    charges,
    counts,
    near_lists,
):
    arguments = (
        multipoles,
        operators.transpose(1, 0, 2),
        parent_locals,
        shifts.transpose(1, 0, 2),
        send_slots.transpose(0, 2, 1),
        lists,
        positions.transpose(1, 0, 2),
        charges,
        counts,
        near_lists,
    )
    vmem = pl.BlockSpec(memory_space=pltpu.VMEM)
    specs = [pl.BlockSpec(memory_space=pltpu.HBM)] * 10
    return pl.pallas_call(
        kernel,
        out_shape=(
            jax.ShapeDtypeStruct((BOX, P2), F32),
            jax.ShapeDtypeStruct((BOX, S), F32),
        ),
        in_specs=specs,
        out_specs=(vmem, vmem),
        scratch_shapes=[pltpu.VMEM(x.shape, x.dtype) for x in arguments]
        + [
            pltpu.VMEM((4, BOX, S), F32),
            pltpu.VMEM((4, BOX, S), F32),
            pltpu.VMEM((BOX, S), F32),
            pltpu.VMEM((BOX, S), F32),
            pltpu.VMEM((64, 4, HALF), BF16),
            pltpu.VMEM((64, 4, HALF), BF16),
            pltpu.VMEM((BOX, FEATURES, S), F32),
            pltpu.VMEM((BOX, FEATURES, S), BF16),
            pltpu.VMEM((BOX, FEATURES, S), BF16),
            pltpu.VMEM((BOX, S, FEATURES), BF16),
            pltpu.VMEM((BOX, S, HALF), F32),
            pltpu.VMEM((BOX, WINDOW, HALF), F32),
            pltpu.VMEM((BOX, S, HALF), F32),
            pltpu.VMEM((BOX, 8, S), F32),
            pltpu.VMEM((BOX, 8, S), F32),
            pltpu.VMEM((BOX, S, OFFSETS), BF16),
            pltpu.VMEM((HALF, BOX, OFFSETS), F32),
            pltpu.VMEM((2, HALF, HALF), F32),
            pltpu.SemaphoreType.DMA((10,)),
            pltpu.SemaphoreType.DMA((2,)),
            pltpu.SemaphoreType.DMA((2,)),
            pltpu.SemaphoreType.DMA,
            pltpu.SemaphoreType.DMA((64,)),
        ],
        compiler_params=pltpu.CompilerParams(
            collective_id=0, has_side_effects=True, vmem_limit_bytes=60 * 2**20
        ),
    )(*arguments)


def solution(mesh):
    placed = (
        P(("zone", "level"), None),
        P(),
        P(("zone", "level"), None),
        P(),
        P(("zone", "level"), None, None),
        P(("zone", "level"), None),
        P(("zone", "level"), None, None),
        P(("zone", "level"), None),
        P(("zone", "level")),
        P(("zone", "level"), None),
    )
    return jax.shard_map(
        per_device,
        mesh=mesh,
        in_specs=placed,
        out_specs=(P(("zone", "level"), None), P(("zone", "level"), None)),
        check_vma=False,
    )
```

time: 60.9 us -> 267 us (4.38)
  the two profiles are of different devices: /device:TPU:16 before, /device:TPU:513 now
where the time goes in v2:
time: 267 us; the launch traced here: 266 us
  Pallas kernels  263 us (99%)
    pallas_call x1, Pallas kernels, per_device(): pl.pallas_call(kernel, out_shape=(jax.ShapeDtypeStruct((BOX, P2), F32), j...  263 us

profile of v2, /device:TPU:513, one launch (start us, length us, event | category | flops | bytes accessed | tf_op | source)
XLA Modules:
  0.0 266.4 jit_solution(6390967343653963729)
XLA Ops:
  0.6 263.2 %shard_map.113 = (f32[16,121]{1,0:T(8,128)}, f32[16,256]{1,0:T(8,128)}) custom-call(bf16[16,121]{1,0:T(8,128)(2,1)} %multipoles_hbm.1, bf16[121,189,121]{2,1,0:T(8,128)(2,1)} %bitcast.4, f32[2,121]{1,0:T(2,128)} %parents_hbm.1, f32[121,8,121]{2,1,0:T(8,128)} %bitcast.5, s32[1,4,64]{2,1,0:T(4,128)} %bitcast.7, s32[16,189]{1,0:T(8,128)} %lists_hbm.1, ...), custom_call_target="tpu_custom_call" | custom-call | tf_op jit(solution)/shard_map/pallas_call | solution.py:424
  263.8 1.3 copy.14
  265.1 1.3 copy.15

commit v3 on v2

--- a/solution.py
+++ b/solution.py
@@ -15,7 +15,7 @@
 OFFSETS = 189
 P2 = 121
 DEPTH = 32
-EXCEPTION = 45
+EXCEPTION = 26
 MESH = pl.DeviceIdType.MESH
 F32 = jnp.float32
 BF16 = jnp.bfloat16
@@ -82,18 +82,15 @@
     first = first_level(level, levels)
     at, after = step(rank, EXCEPTION), step(rank, EXCEPTION + 1)
     base = (rank + first * (1 - at)) * (1 - first * (at - after))
-    distance = (base + 2) // 4
-    side = ((base + 2) % 4) // 2
-    z = (distance + side * (DEPTH - 2 * distance)) % DEPTH
+    upper = step(base, DEPTH)
+    z = base // 2 + upper * (3 * DEPTH // 2 - 1 - 2 * (base // 2))
     return 2 * z + base % 2
 
 
 def rank_of(zone, level, levels):
     first = first_level(level, levels)
     z = zone // 2
-    side = step(z, DEPTH // 2 + 1)
-    distance = z + side * (DEPTH - 2 * z)
-    base = 4 * distance - 2 + 2 * side + zone % 2 + 2 * (1 - step(z, 1))
+    base = 2 * (z + step(z, DEPTH // 2) * (3 * DEPTH // 2 - 1 - 2 * z)) + zone % 2
     inside = step(base, 1)
     return base - first * (inside - step(base, EXCEPTION + 1)) + first * EXCEPTION * (1 - inside)
 
@@ -144,6 +141,7 @@
     back_sem,
     slot_send,
     slot_recv,
+    ready,
 ):
     zone = lax.axis_index("zone")
     level = lax.axis_index("level")
@@ -183,6 +181,20 @@
     def _():
         pl.semaphore_signal(barrier, inc=1, device_id=(zone, level - 1), device_id_type=MESH)
 
+    top = level // (levels - 1)
+
+    @pl.when(rank + 1 - top > 0)
+    def _():
+        pl.semaphore_wait(barrier, rank + 1 - top)
+
+    def greet(r, carry):
+        pl.semaphore_signal(
+            ready, inc=1, device_id=(zone_at(r, level, levels), level), device_id_type=MESH
+        )
+        return carry
+
+    lax.fori_loop(0, rank, greet, 0)
+
     loads["multipoles"].wait()
     loads["slots"].wait()
     own = jnp.concatenate(
@@ -215,16 +227,6 @@
         peer = zone_at(r, level, levels)
         slot_copy(peer, peer, peer).wait_recv()
         return carry
-
-    def answer(r, carry):
-        collect(r, carry)
-        return send(r, carry)
-
-    top = level // (levels - 1)
-
-    @pl.when(rank + 1 - top > 0)
-    def _():
-        pl.semaphore_wait(barrier, rank + 1 - top)
 
     lax.fori_loop(0, rank, send, 0)
     table[zone] = chosen[zone]
@@ -378,8 +380,13 @@
     potential_out[...] = jnp.where(occupied, potential_out[...], 0.0)
     loads["ops"].wait()
 
+    @pl.when(rank < zones - 1)
+    def _():
+        pl.semaphore_wait(ready, zones - 1 - rank)
+
+    lax.fori_loop(rank + 1, zones, send, 0)
     lax.fori_loop(0, rank, collect, 0)
-    lax.fori_loop(rank + 1, zones, answer, 0)
+    lax.fori_loop(rank + 1, zones, collect, 0)
     columns = table[...].reshape(S, HALF).T
     for b in range(BOX):
         gathered[:, b, :] = gathered[:, b, :] + dot(columns, named[b])
@@ -424,8 +431,8 @@
     return pl.pallas_call(
         kernel,
         out_shape=(
-            jax.ShapeDtypeStruct((BOX, P2), F32),
-            jax.ShapeDtypeStruct((BOX, S), F32),
+            pltpu.VMEM((BOX, P2), F32),
+            pltpu.VMEM((BOX, S), F32),
         ),
         in_specs=specs,
         out_specs=(vmem, vmem),
@@ -454,6 +461,7 @@
             pltpu.SemaphoreType.DMA((2,)),
             pltpu.SemaphoreType.DMA,
             pltpu.SemaphoreType.DMA((64,)),
+            pltpu.SemaphoreType.REGULAR,
         ],
         compiler_params=pltpu.CompilerParams(
             collective_id=0, has_side_effects=True, vmem_limit_bytes=60 * 2**20

time: 267 us -> 49.8 us (0.19)
  the two profiles are of different devices: /device:TPU:513 before, /device:TPU:8 now
where the time goes in v3:
time: 49.8 us; the launch traced here: 49.6 us
  Pallas kernels  47.8 us (96%)
  local copies, waits for them, and re-layouts  1.21 us (2%)
  between operations  0.64 us (1%)
    pallas_call x1, Pallas kernels, per_device(): pl.pallas_call(kernel, out_shape=(pltpu.VMEM((BOX, P2), F32), pltpu.VMEM(...  47.8 us
    unnamed x2, local copies, waits for them, and re-layouts  1.21 us

profile of v3, /device:TPU:8, one launch (start us, length us, event | category | flops | bytes accessed | tf_op | source)
XLA Modules:
  0.0 49.6 jit_solution(5848491862395120746)
XLA Ops:
  0.6 47.8 %shard_map.113 = (f32[16,121]{1,0:T(8,128)S(1)}, f32[16,256]{1,0:T(8,128)S(1)}) custom-call(bf16[16,121]{1,0:T(8,128)(2,1)} %multipoles_hbm.1, bf16[121,189,121]{2,1,0:T(8,128)(2,1)} %bitcast.4, f32[2,121]{1,0:T(2,128)} %parents_hbm.1, f32[121,8,121]{2,1,0:T(8,128)} %bitcast.5, s32[1,4,64]{2,1,0:T(4,128)} %bitcast.7, s32[16,189]{1,0:T(8,128)} %lists_hbm.1, ...), custom_call_target="tpu_custom_call" | custom-call | tf_op jit(solution)/shard_map/pallas_call | solution.py:431
  48.4 0.6 %copy.14 = f32[16,121]{1,0:T(8,128)} copy(f32[16,121]{1,0:T(8,128)S(1)} %get-tuple-element.2) | data formatting | bytes 15488
  49.0 0.6 %copy.15 = f32[16,256]{1,0:T(8,128)} copy(f32[16,256]{1,0:T(8,128)S(1)} %get-tuple-element.3) | data formatting | bytes 32768

commit v4 on v3

--- a/solution.py
+++ b/solution.py
@@ -14,8 +14,10 @@
 WINDOW = 48
 OFFSETS = 189
 P2 = 121
-DEPTH = 32
-EXCEPTION = 26
+GROUP = 8
+ZONES = 64
+MOVED = 16
+WORK_FIRST = 48
 MESH = pl.DeviceIdType.MESH
 F32 = jnp.float32
 BF16 = jnp.bfloat16
@@ -70,29 +72,12 @@
         ref[:, k, :] = row
 
 
-def step(a, b):
-    return (a + 64 - b) // 64
-
-
-def first_level(level, levels):
-    return (levels - 1 - level) // (levels - 1)
-
-
-def zone_at(rank, level, levels):
-    first = first_level(level, levels)
-    at, after = step(rank, EXCEPTION), step(rank, EXCEPTION + 1)
-    base = (rank + first * (1 - at)) * (1 - first * (at - after))
-    upper = step(base, DEPTH)
-    z = base // 2 + upper * (3 * DEPTH // 2 - 1 - 2 * (base // 2))
-    return 2 * z + base % 2
-
-
-def rank_of(zone, level, levels):
-    first = first_level(level, levels)
-    z = zone // 2
-    base = 2 * (z + step(z, DEPTH // 2) * (3 * DEPTH // 2 - 1 - 2 * z)) + zone % 2
-    inside = step(base, 1)
-    return base - first * (inside - step(base, EXCEPTION + 1)) + first * EXCEPTION * (1 - inside)
+def over(low, high, body):
+    def one(peer, carry):
+        body(peer)
+        return carry
+
+    lax.fori_loop(low, high, one, 0)
 
 
 def kernel(
@@ -146,11 +131,17 @@
     zone = lax.axis_index("zone")
     level = lax.axis_index("level")
     levels = lax.axis_size("level")
-    zones = lax.axis_size("zone")
-    rank = rank_of(zone, level, levels)
+    group = zone // GROUP
+    top = level // (levels - 1)
+    first = (levels - 1 - level) // (levels - 1)
+    origin = (ZONES - 1 - zone) // (ZONES - 1)
+    moved = first * origin
+    extra = first * (1 - origin) * ((ZONES + MOVED - 1 - zone) // ZONES)
+    before = (extra + moved, zone + MOVED * moved)
+    after = (zone + 1 + (MOVED - 1) * moved, ZONES)
 
     loads = {}
-    for k, (name, source, place) in enumerate(
+    for k, (name, source, held) in enumerate(
         (
             ("multipoles", multipoles_hbm, multipoles),
             ("slots", slots_hbm, slots),
@@ -164,49 +155,25 @@
             ("ops", operators_hbm, ops),
         )
     ):
-        loads[name] = pltpu.make_async_copy(source, place, load_sem.at[k])
+        loads[name] = pltpu.make_async_copy(source, held, load_sem.at[k])
         loads[name].start()
 
     barrier = pltpu.get_barrier_semaphore()
 
-    def tell(r, carry):
+    def signal(semaphore, zone_to, level_to):
         pl.semaphore_signal(
-            barrier, inc=1, device_id=(zone_at(r, level, levels), level), device_id_type=MESH
+            semaphore, inc=1, device_id=(zone_to, level_to), device_id_type=MESH
         )
-        return carry
-
-    lax.fori_loop(rank + 1, zones, tell, 0)
 
     @pl.when(level > 0)
     def _():
-        pl.semaphore_signal(barrier, inc=1, device_id=(zone, level - 1), device_id_type=MESH)
-
-    top = level // (levels - 1)
-
-    @pl.when(rank + 1 - top > 0)
-    def _():
-        pl.semaphore_wait(barrier, rank + 1 - top)
-
-    def greet(r, carry):
-        pl.semaphore_signal(
-            ready, inc=1, device_id=(zone_at(r, level, levels), level), device_id_type=MESH
-        )
-        return carry
-
-    lax.fori_loop(0, rank, greet, 0)
-
-    loads["multipoles"].wait()
-    loads["slots"].wait()
-    own = jnp.concatenate(
-        [multipoles[...], jnp.zeros((BOX, HALF - P2), BF16)], axis=1
-    )
-    reader = iota((S, 64), 0) // 4
-    slot_rows = dot_t(flag(reader == iota((S, 64), 1)), slots[0].astype(F32).astype(BF16))
-    mine = iota((S, 4), 0) % 4 == iota((S, 4), 1)
-    picked = jnp.where(mine, slot_rows, 0.0).astype(BF16)
-    box_of = dot(picked, jnp.ones((4, BOX), BF16))
-    one_hot = flag(box_of == iota((S, BOX), 1).astype(F32))
-    chosen[...] = dot(one_hot, own).reshape(64, 4, HALF).astype(BF16)
+        signal(barrier, zone, level - 1)
+
+    @pl.when(extra == 1)
+    def _():
+        signal(barrier, 0, level)
+
+    over(*after, lambda peer: signal(barrier, peer, level))
 
     def slot_copy(source, place, peer):
         return pltpu.make_async_remote_copy(
@@ -218,18 +185,26 @@
             device_id_type=MESH,
         )
 
-    def send(r, carry):
-        peer = zone_at(r, level, levels)
+    def send(peer):
         slot_copy(peer, zone, peer).start()
-        return carry
-
-    def collect(r, carry):
-        peer = zone_at(r, level, levels)
+
+    def send_early(peer):
+        send(peer)
+        signal(ready.at[group + GROUP * moved], peer, level)
+
+    def collect(peer):
         slot_copy(peer, peer, peer).wait_recv()
-        return carry
-
-    lax.fori_loop(0, rank, send, 0)
-    table[zone] = chosen[zone]
+
+    loads["multipoles"].wait()
+    loads["slots"].wait()
+    own = jnp.concatenate([multipoles[...], jnp.zeros((BOX, HALF - P2), BF16)], axis=1)
+    reader = iota((S, ZONES), 0) // 4
+    slot_rows = dot_t(flag(reader == iota((S, ZONES), 1)), slots[0].astype(F32).astype(BF16))
+    mine = iota((S, 4), 0) % 4 == iota((S, 4), 1)
+    picked = jnp.where(mine, slot_rows, 0.0).astype(BF16)
+    box_of = dot(picked, jnp.ones((4, BOX), BF16))
+    one_hot = flag(box_of == iota((S, BOX), 1).astype(F32))
+    chosen[...] = dot(one_hot, own).reshape(ZONES, 4, HALF).astype(BF16)
 
     for name in ("counts", "positions", "charges"):
         loads[name].wait()
@@ -259,32 +234,7 @@
         device_id_type=MESH,
     )
 
-    @pl.when(level < levels - 1)
-    def _():
-        halo_copy.start()
-
     middle = [jnp.sum(halo_out[c, :, 0:1], axis=0, keepdims=True) * (1.0 / BOX) for c in range(3)]
-    offsets = [halo_out[c] - middle[c] for c in range(3)]
-    identity = flag(iota((S, S), 0) == iota((S, S), 1))
-    write_features(features, offsets, True)
-
-    def prepare(b, carry):
-        targets[b] = dot_t(identity, features[b].astype(BF16)).astype(BF16)
-        row = jnp.broadcast_to(halo_out[3, pl.ds(b, 1), :], (HALF, S))
-        charge_columns[b] = row.T
-        sums[b] = jnp.zeros((S, HALF), F32)
-        return carry
-
-    lax.fori_loop(0, BOX, prepare, 0)
-    write_features(features, offsets, False)
-    sources[...] = features[...].astype(BF16)
-    own_sums[...] = jnp.zeros_like(own_sums)
-    below_sums[...] = jnp.zeros_like(below_sums)
-    loads["near"].wait()
-    hits = flag(near[...][:, None, :] == iota((BOX, WINDOW, NEAR), 1))
-    present[...] = dot(
-        hits.reshape(BOX * WINDOW, NEAR), jnp.ones((NEAR, HALF), BF16)
-    ).reshape(BOX, WINDOW, HALF)
 
     def block(b, n, shift, side, charge, other):
         y = lax.rsqrt(dot(targets[b], side[n]))
@@ -328,7 +278,81 @@
             block(code(x, y), code(x_next, y_next), 0, below, halo_in, below_sums)
         return carry
 
-    lax.fori_loop(0, 3, own_pairs, 0)
+    def prepare_and_pair():
+        offsets = [halo_out[c] - middle[c] for c in range(3)]
+        identity = flag(iota((S, S), 0) == iota((S, S), 1))
+        write_features(features, offsets, True)
+
+        def prepare(b, carry):
+            targets[b] = dot_t(identity, features[b].astype(BF16)).astype(BF16)
+            row = jnp.broadcast_to(halo_out[3, pl.ds(b, 1), :], (HALF, S))
+            charge_columns[b] = row.T
+            sums[b] = jnp.zeros((S, HALF), F32)
+            return carry
+
+        lax.fori_loop(0, BOX, prepare, 0)
+        write_features(features, offsets, False)
+        sources[...] = features[...].astype(BF16)
+        own_sums[...] = jnp.zeros_like(own_sums)
+        below_sums[...] = jnp.zeros_like(below_sums)
+        loads["near"].wait()
+        hits = flag(near[...][:, None, :] == iota((BOX, WINDOW, NEAR), 1))
+        present[...] = dot(
+            hits.reshape(BOX * WINDOW, NEAR), jnp.ones((NEAR, HALF), BF16)
+        ).reshape(BOX, WINDOW, HALF)
+
+        lax.fori_loop(0, 3, own_pairs, 0)
+
+    def name_members():
+        loads["lists"].wait()
+        own_columns = own.T
+        entry = BOX + iota((S, OFFSETS), 0)
+        for b in range(BOX):
+            row = lists[b : b + 1, :]
+            named[b] = flag(entry == row)
+            gathered[:, b, :] = dot(own_columns, flag(iota((BOX, OFFSETS), 0) == row))
+
+        loads["parents"].wait()
+        loads["shifts"].wait()
+        for g in range(2):
+            row = jnp.concatenate([parents[g : g + 1, :], jnp.zeros((1, HALF - P2), F32)], axis=1)
+            parent_columns[g] = jnp.broadcast_to(row, (HALF, HALF)).T
+        for g in range(2):
+            total = jnp.zeros((8, P2), F32)
+            for p in range(P2):
+                total = total + parent_columns[g, p : p + 1, :P2] * shifts[p]
+            local_out[8 * g : 8 * g + 8, :] = total
+
+    def send_first():
+        count_before = before[1] - before[0]
+
+        @pl.when(count_before + 1 - top > 0)
+        def _():
+            pl.semaphore_wait(barrier, count_before + 1 - top)
+
+        over(*before, send_early)
+        table[zone] = chosen[zone]
+
+        @pl.when(level < levels - 1)
+        def _():
+            halo_copy.start()
+
+    here = 1 - (zone + ZONES - WORK_FIRST) // ZONES
+
+    def phase(k, carry):
+        @pl.when(k == here)
+        def _():
+            prepare_and_pair()
+
+        @pl.when(k == 1 - here)
+        def _():
+            send_first()
+
+        return carry
+
+    lax.fori_loop(0, 2, phase, 0)
+    lax.fori_loop(0, 4, self_pairs, 0)
+    name_members()
 
     @pl.when(level > 0)
     def _():
@@ -339,26 +363,6 @@
         back_out[...] = jnp.sum(below_sums[...], axis=1)
         back_copy.start()
 
-    lax.fori_loop(0, 4, self_pairs, 0)
-
-    loads["lists"].wait()
-    own_columns = own.T
-    for b in range(BOX):
-        row = lists[b : b + 1, :]
-        named[b] = flag(iota((S, OFFSETS), 0) + BOX == row)
-        gathered[:, b, :] = dot(own_columns, flag(iota((BOX, OFFSETS), 0) == row))
-
-    loads["parents"].wait()
-    loads["shifts"].wait()
-    for g in range(2):
-        row = jnp.concatenate([parents[g : g + 1, :], jnp.zeros((1, HALF - P2), F32)], axis=1)
-        parent_columns[g] = jnp.broadcast_to(row, (HALF, HALF)).T
-    for g in range(2):
-        total = jnp.zeros((8, P2), F32)
-        for p in range(P2):
-            total = total + parent_columns[g, p : p + 1, :P2] * shifts[p]
-        local_out[8 * g : 8 * g + 8, :] = total
-
     def finish(b, carry):
         mine = jnp.sum(sums[b].T, axis=0, keepdims=True)
         theirs = jnp.sum(own_sums[b], axis=0, keepdims=True)
@@ -380,13 +384,27 @@
     potential_out[...] = jnp.where(occupied, potential_out[...], 0.0)
     loads["ops"].wait()
 
-    @pl.when(rank < zones - 1)
-    def _():
-        pl.semaphore_wait(ready, zones - 1 - rank)
-
-    lax.fori_loop(rank + 1, zones, send, 0)
-    lax.fori_loop(0, rank, collect, 0)
-    lax.fori_loop(rank + 1, zones, collect, 0)
+    in_group = (GROUP - 1 - zone % GROUP) * (1 - moved)
+
+    @pl.when(in_group > 0)
+    def _():
+        pl.semaphore_wait(ready.at[group], in_group)
+        over(zone + 1, zone + 1 + in_group, send)
+
+    @pl.when(extra == 1)
+    def _():
+        pl.semaphore_wait(ready.at[GROUP], 1)
+        send(0)
+
+    for g in (1, 2, 3, 7, 6, 5, 4):
+
+        @pl.when(group + moved < g)
+        def _():
+            pl.semaphore_wait(ready.at[g], GROUP)
+            over(GROUP * g, GROUP * g + GROUP, send)
+
+    over(0, zone, collect)
+    over(zone + 1, ZONES, collect)
     columns = table[...].reshape(S, HALF).T
     for b in range(BOX):
         gathered[:, b, :] = gathered[:, b, :] + dot(columns, named[b])
@@ -399,7 +417,8 @@
 
     far = lax.fori_loop(0, P2 // 11, translate, jnp.zeros((BOX, P2), F32), unroll=True)
     local_out[...] = local_out[...] + far
-    pltpu.make_async_copy(chosen.at[pl.ds(1, 63)], chosen.at[pl.ds(1, 63)], slot_send).wait()
+    whole = chosen.at[pl.ds(1, ZONES - 1)]
+    pltpu.make_async_copy(whole, whole, slot_send).wait()
 
 
 def per_device(
@@ -442,8 +461,8 @@
             pltpu.VMEM((4, BOX, S), F32),
             pltpu.VMEM((BOX, S), F32),
             pltpu.VMEM((BOX, S), F32),
-            pltpu.VMEM((64, 4, HALF), BF16),
-            pltpu.VMEM((64, 4, HALF), BF16),
+            pltpu.VMEM((ZONES, 4, HALF), BF16),
+            pltpu.VMEM((ZONES, 4, HALF), BF16),
             pltpu.VMEM((BOX, FEATURES, S), F32),
             pltpu.VMEM((BOX, FEATURES, S), BF16),
             pltpu.VMEM((BOX, FEATURES, S), BF16),
@@ -460,8 +479,8 @@
             pltpu.SemaphoreType.DMA((2,)),
             pltpu.SemaphoreType.DMA((2,)),
             pltpu.SemaphoreType.DMA,
-            pltpu.SemaphoreType.DMA((64,)),
-            pltpu.SemaphoreType.REGULAR,
+            pltpu.SemaphoreType.DMA((ZONES,)),
+            pltpu.SemaphoreType.REGULAR((GROUP + 1,)),
         ],
         compiler_params=pltpu.CompilerParams(
             collective_id=0, has_side_effects=True, vmem_limit_bytes=60 * 2**20

time: 49.8 us -> 44.8 us (0.90)
  the two profiles are of different devices: /device:TPU:8 before, /device:TPU:963 now
where the time goes in v4:
time: 44.8 us; the launch traced here: 44.6 us
  Pallas kernels  42.8 us (96%)
  local copies, waits for them, and re-layouts  1.21 us (3%)
  between operations  0.64 us (1%)
    pallas_call x1, Pallas kernels, per_device(): pl.pallas_call(kernel, out_shape=(pltpu.VMEM((BOX, P2), F32), pltpu.VMEM(...  42.8 us
    unnamed x2, local copies, waits for them, and re-layouts  1.21 us

profile of v4, /device:TPU:963, one launch (start us, length us, event | category | flops | bytes accessed | tf_op | source)
XLA Modules:
  0.0 44.6 jit_solution(684454673000260228)
XLA Ops:
  0.6 42.8 %shard_map.113 = (f32[16,121]{1,0:T(8,128)S(1)}, f32[16,256]{1,0:T(8,128)S(1)}) custom-call(bf16[16,121]{1,0:T(8,128)(2,1)} %multipoles_hbm.1, bf16[121,189,121]{2,1,0:T(8,128)(2,1)} %bitcast.4, f32[2,121]{1,0:T(2,128)} %parents_hbm.1, f32[121,8,121]{2,1,0:T(8,128)} %bitcast.5, s32[1,4,64]{2,1,0:T(4,128)} %bitcast.7, s32[16,189]{1,0:T(8,128)} %lists_hbm.1, ...), custom_call_target="tpu_custom_call" | custom-call | tf_op jit(solution)/shard_map/pallas_call | solution.py:450
  43.4 0.6 %copy.14 = f32[16,121]{1,0:T(8,128)} copy(f32[16,121]{1,0:T(8,128)S(1)} %get-tuple-element.2) | data formatting | bytes 15488
  44.0 0.6 %copy.15 = f32[16,256]{1,0:T(8,128)} copy(f32[16,256]{1,0:T(8,128)S(1)} %get-tuple-element.3) | data formatting | bytes 32768

commit v5 on v4

--- a/solution.py
+++ b/solution.py
@@ -17,6 +17,7 @@
 GROUP = 8
 ZONES = 64
 MOVED = 16
+FAR = 32
 WORK_FIRST = 48
 MESH = pl.DeviceIdType.MESH
 F32 = jnp.float32
@@ -127,6 +128,11 @@
     slot_send,
     slot_recv,
     ready,
+    inbound,
+    outbound,
+    inbound_recv,
+    outbound_recv,
+    relay_send,
 ):
     zone = lax.axis_index("zone")
     level = lax.axis_index("level")
@@ -137,7 +143,9 @@
     origin = (ZONES - 1 - zone) // (ZONES - 1)
     moved = first * origin
     extra = first * (1 - origin) * ((ZONES + MOVED - 1 - zone) // ZONES)
-    before = (extra + moved, zone + MOVED * moved)
+    far = first * ((group + 4) // GROUP - (group + 3) // GROUP)
+    relay = first * ((zone + ZONES - 1) // ZONES - (zone + ZONES - 2) // ZONES)
+    before = (extra + moved + far, zone + MOVED * moved)
     after = (zone + 1 + (MOVED - 1) * moved, ZONES)
 
     loads = {}
@@ -156,7 +164,9 @@
         )
     ):
         loads[name] = pltpu.make_async_copy(source, held, load_sem.at[k])
-        loads[name].start()
+
+    loads["slots"].start()
+    loads["multipoles"].start()
 
     barrier = pltpu.get_barrier_semaphore()
 
@@ -165,6 +175,15 @@
             semaphore, inc=1, device_id=(zone_to, level_to), device_id_type=MESH
         )
 
+    def tell(low, high):
+        over(0, high - low, lambda k: signal(barrier, high - 1 - k, level))
+
+    @pl.when(moved == 1)
+    def _():
+        tell(FAR + GROUP, ZONES)
+
+    tell(after[0], ZONES - FAR * moved)
+
     @pl.when(level > 0)
     def _():
         signal(barrier, zone, level - 1)
@@ -173,14 +192,15 @@
     def _():
         signal(barrier, 0, level)
 
-    over(*after, lambda peer: signal(barrier, peer, level))
+    for name in ("counts", "positions", "charges", "near", "lists", "parents", "shifts", "ops"):
+        loads[name].start()
 
     def slot_copy(source, place, peer):
         return pltpu.make_async_remote_copy(
             src_ref=chosen.at[source],
             dst_ref=table.at[place],
             send_sem=slot_send,
-            recv_sem=slot_recv.at[place],
+            recv_sem=slot_recv,
             device_id=(peer, level),
             device_id_type=MESH,
         )
@@ -188,12 +208,45 @@
     def send(peer):
         slot_copy(peer, zone, peer).start()
 
+    def greet(peer):
+        signal(ready.at[group + GROUP * moved], peer, level)
+
     def send_early(peer):
         send(peer)
-        signal(ready.at[group + GROUP * moved], peer, level)
-
-    def collect(peer):
-        slot_copy(peer, peer, peer).wait_recv()
+        greet(peer)
+
+    def to_relay(source, target, receive):
+        return pltpu.make_async_remote_copy(
+            src_ref=source,
+            dst_ref=target,
+            send_sem=slot_send,
+            recv_sem=receive,
+            device_id=(1, level),
+            device_id_type=MESH,
+        )
+
+    inward = to_relay(chosen.at[0], inbound.at[zone % GROUP], inbound_recv.at[zone % GROUP])
+    outward = to_relay(chosen.at[pl.ds(FAR, GROUP)], outbound, outbound_recv)
+
+    def pass_in():
+        return pltpu.make_async_remote_copy(
+            src_ref=inbound,
+            dst_ref=table.at[pl.ds(FAR, GROUP)],
+            send_sem=relay_send,
+            recv_sem=slot_recv,
+            device_id=(0, level),
+            device_id_type=MESH,
+        )
+
+    def pass_out(k):
+        return pltpu.make_async_remote_copy(
+            src_ref=outbound.at[k],
+            dst_ref=table.at[0],
+            send_sem=relay_send,
+            recv_sem=slot_recv,
+            device_id=(FAR + k, level),
+            device_id_type=MESH,
+        )
 
     loads["multipoles"].wait()
     loads["slots"].wait()
@@ -330,7 +383,23 @@
         def _():
             pl.semaphore_wait(barrier, count_before + 1 - top)
 
-        over(*before, send_early)
+        @pl.when(here == 1)
+        def _():
+            over(*before, send_early)
+
+        @pl.when(here == 0)
+        def _():
+            over(*before, greet)
+            over(*before, send)
+
+        @pl.when(far == 1)
+        def _():
+            inward.start()
+
+        @pl.when(moved == 1)
+        def _():
+            outward.start()
+
         table[zone] = chosen[zone]
 
         @pl.when(level < levels - 1)
@@ -396,15 +465,28 @@
         pl.semaphore_wait(ready.at[GROUP], 1)
         send(0)
 
-    for g in (1, 2, 3, 7, 6, 5, 4):
-
-        @pl.when(group + moved < g)
+    for g in range(1, GROUP):
+
+        @pl.when(group + (4 if g == 4 else 1) * moved < g)
         def _():
             pl.semaphore_wait(ready.at[g], GROUP)
             over(GROUP * g, GROUP * g + GROUP, send)
 
-    over(0, zone, collect)
-    over(zone + 1, ZONES, collect)
+    @pl.when(relay == 1)
+    def _():
+        outward.wait_recv()
+
+        def pass_one(k, carry):
+            pass_out(k).start()
+            return carry
+
+        lax.fori_loop(0, GROUP, pass_one, 0)
+        for k in range(GROUP):
+            to_relay(chosen.at[0], inbound.at[k], inbound_recv.at[k]).wait_recv()
+        pass_in().start()
+
+    others = table.at[pl.ds(1, ZONES - 1)]
+    pltpu.make_async_copy(others, others, slot_recv).wait()
     columns = table[...].reshape(S, HALF).T
     for b in range(BOX):
         gathered[:, b, :] = gathered[:, b, :] + dot(columns, named[b])
@@ -419,6 +501,11 @@
     local_out[...] = local_out[...] + far
     whole = chosen.at[pl.ds(1, ZONES - 1)]
     pltpu.make_async_copy(whole, whole, slot_send).wait()
+
+    @pl.when(relay == 1)
+    def _():
+        passed = chosen.at[pl.ds(0, 2 * GROUP)]
+        pltpu.make_async_copy(passed, passed, relay_send).wait()
 
 
 def per_device(
@@ -479,8 +566,13 @@
             pltpu.SemaphoreType.DMA((2,)),
             pltpu.SemaphoreType.DMA((2,)),
             pltpu.SemaphoreType.DMA,
-            pltpu.SemaphoreType.DMA((ZONES,)),
+            pltpu.SemaphoreType.DMA,
             pltpu.SemaphoreType.REGULAR((GROUP + 1,)),
+            pltpu.VMEM((GROUP, 4, HALF), BF16),
+            pltpu.VMEM((GROUP, 4, HALF), BF16),
+            pltpu.SemaphoreType.DMA((GROUP,)),
+            pltpu.SemaphoreType.DMA,
+            pltpu.SemaphoreType.DMA,
         ],
         compiler_params=pltpu.CompilerParams(
             collective_id=0, has_side_effects=True, vmem_limit_bytes=60 * 2**20

time: 44.8 us -> 44.2 us (0.987)
  the two profiles are of different devices: /device:TPU:963 before, /device:TPU:993 now
where the time goes in v5:
time: 44.2 us; the launch traced here: 44 us
  Pallas kernels  42.1 us (95%)
  local copies, waits for them, and re-layouts  1.21 us (3%)
  between operations  0.64 us (1%)
    pallas_call x1, Pallas kernels, per_device(): pl.pallas_call(kernel, out_shape=(pltpu.VMEM((BOX, P2), F32), pltpu.VMEM(...  42.1 us
    unnamed x2, local copies, waits for them, and re-layouts  1.21 us

profile of v5, /device:TPU:993, one launch (start us, length us, event | category | flops | bytes accessed | tf_op | source)
XLA Modules:
  0.0 44.0 jit_solution(6582600119257838648)
XLA Ops:
  0.6 42.1 %shard_map.113 = (f32[16,121]{1,0:T(8,128)S(1)}, f32[16,256]{1,0:T(8,128)S(1)}) custom-call(bf16[16,121]{1,0:T(8,128)(2,1)} %multipoles_hbm.1, bf16[121,189,121]{2,1,0:T(8,128)(2,1)} %bitcast.4, f32[2,121]{1,0:T(2,128)} %parents_hbm.1, f32[121,8,121]{2,1,0:T(8,128)} %bitcast.5, s32[1,4,64]{2,1,0:T(4,128)} %bitcast.7, s32[16,189]{1,0:T(8,128)} %lists_hbm.1, ...), custom_call_target="tpu_custom_call" | custom-call | tf_op jit(solution)/shard_map/pallas_call | solution.py:537
  42.8 0.6 %copy.14 = f32[16,121]{1,0:T(8,128)} copy(f32[16,121]{1,0:T(8,128)S(1)} %get-tuple-element.2) | data formatting | bytes 15488
  43.4 0.6 %copy.15 = f32[16,256]{1,0:T(8,128)} copy(f32[16,256]{1,0:T(8,128)S(1)} %get-tuple-element.3) | data formatting | bytes 32768

commit v6 on v5

--- a/solution.py
+++ b/solution.py
@@ -18,6 +18,8 @@
 ZONES = 64
 MOVED = 16
 FAR = 32
+LODGED = 24
+LAST = 56
 WORK_FIRST = 48
 MESH = pl.DeviceIdType.MESH
 F32 = jnp.float32
@@ -133,6 +135,9 @@
     inbound_recv,
     outbound_recv,
     relay_send,
+    held_rows,
+    held_recv,
+    held_send,
 ):
     zone = lax.axis_index("zone")
     level = lax.axis_index("level")
@@ -145,6 +150,8 @@
     extra = first * (1 - origin) * ((ZONES + MOVED - 1 - zone) // ZONES)
     far = first * ((group + 4) // GROUP - (group + 3) // GROUP)
     relay = first * ((zone + ZONES - 1) // ZONES - (zone + ZONES - 2) // ZONES)
+    lodger = (group + 5) // GROUP - (group + 4) // GROUP
+    host = (GROUP - 1 - group) // (GROUP - 1)
     before = (extra + moved + far, zone + MOVED * moved)
     after = (zone + 1 + (MOVED - 1) * moved, ZONES)
 
@@ -228,6 +235,25 @@
     inward = to_relay(chosen.at[0], inbound.at[zone % GROUP], inbound_recv.at[zone % GROUP])
     outward = to_relay(chosen.at[pl.ds(FAR, GROUP)], outbound, outbound_recv)
 
+    lodge = pltpu.make_async_remote_copy(
+        src_ref=chosen.at[pl.ds(LAST, GROUP)],
+        dst_ref=held_rows,
+        send_sem=slot_send,
+        recv_sem=held_recv,
+        device_id=(zone % GROUP, level),
+        device_id_type=MESH,
+    )
+
+    def pass_held(k):
+        return pltpu.make_async_remote_copy(
+            src_ref=held_rows.at[k],
+            dst_ref=table.at[LODGED + zone % GROUP],
+            send_sem=held_send,
+            recv_sem=slot_recv,
+            device_id=(LAST + k, level),
+            device_id_type=MESH,
+        )
+
     def pass_in():
         return pltpu.make_async_remote_copy(
             src_ref=inbound,
@@ -392,6 +418,10 @@
             over(*before, greet)
             over(*before, send)
 
+        @pl.when(lodger == 1)
+        def _():
+            lodge.start()
+
         @pl.when(far == 1)
         def _():
             inward.start()
@@ -422,6 +452,33 @@
     lax.fori_loop(0, 2, phase, 0)
     lax.fori_loop(0, 4, self_pairs, 0)
     name_members()
+
+    late = (zone + ZONES - FAR) // ZONES
+
+    def answer_all():
+        in_group = (GROUP - 1 - zone % GROUP) * (1 - moved)
+
+        @pl.when(in_group > 0)
+        def _():
+            pl.semaphore_wait(ready.at[group], in_group)
+            over(zone + 1, zone + 1 + in_group, send)
+
+        @pl.when(extra == 1)
+        def _():
+            pl.semaphore_wait(ready.at[GROUP], 1)
+            send(0)
+
+        for g in range(1, GROUP):
+
+            @pl.when(group + (4 if g == 4 else 1) * moved < g)
+            def _():
+                pl.semaphore_wait(ready.at[g], GROUP)
+                skip = GROUP * lodger if g == GROUP - 1 else 0
+                over(GROUP * g + skip, GROUP * g + GROUP, send)
+
+    @pl.when(late == 1)
+    def _():
+        answer_all()
 
     @pl.when(level > 0)
     def _():
@@ -453,24 +510,9 @@
     potential_out[...] = jnp.where(occupied, potential_out[...], 0.0)
     loads["ops"].wait()
 
-    in_group = (GROUP - 1 - zone % GROUP) * (1 - moved)
-
-    @pl.when(in_group > 0)
-    def _():
-        pl.semaphore_wait(ready.at[group], in_group)
-        over(zone + 1, zone + 1 + in_group, send)
-
-    @pl.when(extra == 1)
-    def _():
-        pl.semaphore_wait(ready.at[GROUP], 1)
-        send(0)
-
-    for g in range(1, GROUP):
-
-        @pl.when(group + (4 if g == 4 else 1) * moved < g)
-        def _():
-            pl.semaphore_wait(ready.at[g], GROUP)
-            over(GROUP * g, GROUP * g + GROUP, send)
+    @pl.when(late == 0)
+    def _():
+        answer_all()
 
     @pl.when(relay == 1)
     def _():
@@ -484,6 +526,16 @@
         for k in range(GROUP):
             to_relay(chosen.at[0], inbound.at[k], inbound_recv.at[k]).wait_recv()
         pass_in().start()
+
+    @pl.when(host == 1)
+    def _():
+        lodge.wait_recv()
+
+        def pass_one(k, carry):
+            pass_held(k).start()
+            return carry
+
+        lax.fori_loop(0, GROUP, pass_one, 0)
 
     others = table.at[pl.ds(1, ZONES - 1)]
     pltpu.make_async_copy(others, others, slot_recv).wait()
@@ -501,6 +553,11 @@
     local_out[...] = local_out[...] + far
     whole = chosen.at[pl.ds(1, ZONES - 1)]
     pltpu.make_async_copy(whole, whole, slot_send).wait()
+
+    @pl.when(host == 1)
+    def _():
+        passed = chosen.at[pl.ds(0, GROUP)]
+        pltpu.make_async_copy(passed, passed, held_send).wait()
 
     @pl.when(relay == 1)
     def _():
@@ -573,6 +630,9 @@
             pltpu.SemaphoreType.DMA((GROUP,)),
             pltpu.SemaphoreType.DMA,
             pltpu.SemaphoreType.DMA,
+            pltpu.VMEM((GROUP, 4, HALF), BF16),
+            pltpu.SemaphoreType.DMA,
+            pltpu.SemaphoreType.DMA,
         ],
         compiler_params=pltpu.CompilerParams(
             collective_id=0, has_side_effects=True, vmem_limit_bytes=60 * 2**20

time: 44.2 us -> 40.3 us (0.912)
  the two profiles are of different devices: /device:TPU:993 before, /device:TPU:1 now
where the time goes in v6:
time: 40.3 us; the launch traced here: 40.1 us
  Pallas kernels  38.3 us (95%)
  local copies, waits for them, and re-layouts  1.21 us (3%)
  between operations  0.64 us (2%)
    pallas_call x1, Pallas kernels, per_device(): pl.pallas_call(kernel, out_shape=(pltpu.VMEM((BOX, P2), F32), pltpu.VMEM(...  38.3 us
    unnamed x2, local copies, waits for them, and re-layouts  1.21 us

profile of v6, /device:TPU:1, one launch (start us, length us, event | category | flops | bytes accessed | tf_op | source)
XLA Modules:
  0.0 40.1 jit_solution(376113334932183256)
XLA Ops:
  0.6 38.3 %shard_map.113 = (f32[16,121]{1,0:T(8,128)S(1)}, f32[16,256]{1,0:T(8,128)S(1)}) custom-call(bf16[16,121]{1,0:T(8,128)(2,1)} %multipoles_hbm.1, bf16[121,189,121]{2,1,0:T(8,128)(2,1)} %bitcast.4, f32[2,121]{1,0:T(2,128)} %parents_hbm.1, f32[121,8,121]{2,1,0:T(8,128)} %bitcast.5, s32[1,4,64]{2,1,0:T(4,128)} %bitcast.7, s32[16,189]{1,0:T(8,128)} %lists_hbm.1, ...), custom_call_target="tpu_custom_call" | custom-call | tf_op jit(solution)/shard_map/pallas_call | solution.py:594
  38.9 0.6 %copy.14 = f32[16,121]{1,0:T(8,128)} copy(f32[16,121]{1,0:T(8,128)S(1)} %get-tuple-element.2) | data formatting | bytes 15488
  39.5 0.6 %copy.15 = f32[16,256]{1,0:T(8,128)} copy(f32[16,256]{1,0:T(8,128)S(1)} %get-tuple-element.3) | data formatting | bytes 32768
